TPU v7x, 32 devices: a whole 2x2x4 slice. The times are simulated.
32 devices in a mesh: view: 16 (over z, x, core), tok: 2 (over y).
Axes of the slice: x: 2, y: 2, z: 4, core: 2. Of those that a mesh axis runs over, the one named last changes fastest.
Arguments:
- queries: bfloat16 [48, 98, 1024], P('view', 'tok'), may hold values from -6 to 6
- keys: bfloat16 [48, 98, 1024], P('view', 'tok'), may hold values from -6 to 6
- values: bfloat16 [48, 98, 1024], P('view', 'tok'), may hold values from -6 to 6
- grad_out: bfloat16 [48, 98, 1024], P('view', 'tok'), may hold values from -6 to 6
Outputs:
- attended: bfloat16 [48, 98, 1024], P('view', 'tok')
- query_grad: bfloat16 [48, 98, 1024], P('view', 'tok')
- key_grad: bfloat16 [48, 98, 1024], P('view', 'tok')
- value_grad: bfloat16 [48, 98, 1024], P('view', 'tok')
All inputs are finite; a program needn't handle non-finite values.
Results may differ from a plain program's by a relative error of at most 0.03.
Values may be sent and summed in bfloat16 or wider, within the bound.
A program may use at most 128 MiB of HBM per device.

v0:
```python
import math

import jax
import jax.numpy as jnp
from jax import lax
from jax.sharding import PartitionSpec as P

HEADS = 16


def padded(value, sides, width):
    for axis, dim in sides:
        size, length = (lax.axis_size(axis), value.shape[dim])
        up = [(i, (i + 1) % size) for i in range(size)]
        down = [(j, i) for i, j in up]
        last = lax.slice_in_dim(value, length - width, length, axis=dim)
        leading = lax.slice_in_dim(value, 0, width, axis=dim)
        before = lax.ppermute(last, axis, up)
        after = lax.ppermute(leading, axis, down)
        value = jnp.concatenate([before, value, after], axis=dim)
    return value


def attend_view(query_view, grad_view, key_window, value_window, score_scale):
    f32 = jnp.float32
    scores = (
        jnp.einsum("qhd,khd->hqk", query_view, key_window, preferred_element_type=f32) * score_scale
    )
    row_max = jnp.max(scores, axis=-1, keepdims=True)
    log_total = row_max[..., 0] + jnp.log(jnp.sum(jnp.exp(scores - row_max), axis=-1))
    probs = jnp.exp(scores - log_total[..., None])
    probs_bf = probs.astype(jnp.bfloat16)
    attended = jnp.einsum(
        "hqk,khd->qhd", probs_bf, value_window, preferred_element_type=f32
    ).astype(jnp.bfloat16)
    row_delta = jnp.sum(grad_view.astype(f32) * attended.astype(f32), axis=-1).T
    grad_probs = jnp.einsum("qhd,khd->hqk", grad_view, value_window, preferred_element_type=f32)
    grad_bf = (probs * (grad_probs - row_delta[..., None])).astype(jnp.bfloat16)
    query_grad = (
        jnp.einsum("hqk,khd->qhd", grad_bf, key_window, preferred_element_type=f32) * score_scale
    )
    return (attended, query_grad.astype(jnp.bfloat16), log_total, row_delta)


def tokens_layout(queries, keys, values, grad_out):
    view_count, shard_toks, model_width = queries.shape
    head_dim = model_width // HEADS
    score_scale = 1.0 / math.sqrt(head_dim)
    f32 = jnp.float32
    kv_stack = jnp.stack([keys, values])
    gathered = lax.all_gather(kv_stack, "tok", axis=2, tiled=True)
    extended = padded(gathered, (("view", 1),), 1)
    ext_keys = extended[0]
    ext_values = extended[1]
    view_toks = ext_keys.shape[1]

    def forward_view(view_index):
        key_window = lax.dynamic_slice_in_dim(ext_keys, view_index, 3, 0).reshape(
            3 * view_toks, HEADS, head_dim
        )
        value_window = lax.dynamic_slice_in_dim(ext_values, view_index, 3, 0).reshape(
            3 * view_toks, HEADS, head_dim
        )
        query_view = lax.dynamic_index_in_dim(queries, view_index, 0, False).reshape(
            shard_toks, HEADS, head_dim
        )
        grad_view = lax.dynamic_index_in_dim(grad_out, view_index, 0, False).reshape(
            shard_toks, HEADS, head_dim
        )
        attended, query_grad, log_total, row_delta = attend_view(
            query_view, grad_view, key_window, value_window, score_scale
        )
        return (
            attended.reshape(shard_toks, model_width),
            query_grad.reshape(shard_toks, model_width),
            log_total,
            row_delta,
        )

    attended, query_grad, log_totals, row_deltas = lax.map(forward_view, jnp.arange(view_count))
    rim_rows = padded(jnp.stack([queries, grad_out, attended]), (("view", 1),), 1)
    total_ext = padded(log_totals, (("view", 0),), 1)
    query_ext = rim_rows[0]
    grad_ext = rim_rows[1]
    product = grad_ext.astype(f32) * rim_rows[2].astype(f32)
    delta_ext = jnp.sum(
        product.reshape(view_count + 2, shard_toks, HEADS, head_dim), axis=-1
    ).transpose(0, 2, 1)
    own_keys = ext_keys[1 : view_count + 1]
    own_values = ext_values[1 : view_count + 1]
    row_count = shard_toks * lax.axis_size("tok")

    def one_view(view_index):
        query_rows = lax.dynamic_slice_in_dim(query_ext, view_index, 3, 0).reshape(
            3 * shard_toks, HEADS, head_dim
        )
        grad_rows = lax.dynamic_slice_in_dim(grad_ext, view_index, 3, 0).reshape(
            3 * shard_toks, HEADS, head_dim
        )
        total_rows = (
            lax.dynamic_slice_in_dim(total_ext, view_index, 3, 0)
            .transpose(1, 0, 2)
            .reshape(HEADS, 3 * shard_toks)
        )
        delta_rows = (
            lax.dynamic_slice_in_dim(delta_ext, view_index, 3, 0)
            .transpose(1, 0, 2)
            .reshape(HEADS, 3 * shard_toks)
        )
        key_view = lax.dynamic_index_in_dim(own_keys, view_index, 0, False)
        value_view = lax.dynamic_index_in_dim(own_values, view_index, 0, False)
        key_rows = key_view.reshape(row_count, HEADS, head_dim)
        value_rows = value_view.reshape(row_count, HEADS, head_dim)
        scores = (
            jnp.einsum("qhd,khd->hqk", query_rows, key_rows, preferred_element_type=f32)
            * score_scale
        )
        probs = jnp.exp(scores - total_rows[..., None])
        probs_bf = probs.astype(jnp.bfloat16)
        grad_probs = jnp.einsum("qhd,khd->hqk", grad_rows, value_rows, preferred_element_type=f32)
        grad_bf = (probs * (grad_probs - delta_rows[..., None])).astype(jnp.bfloat16)
        key_term = (
            jnp.einsum("hqk,qhd->khd", grad_bf, query_rows, preferred_element_type=f32)
            * score_scale
        )
        value_term = jnp.einsum("hqk,qhd->khd", probs_bf, grad_rows, preferred_element_type=f32)
        return jnp.stack(
            [key_term.reshape(row_count, model_width), value_term.reshape(row_count, model_width)],
            1,
        )

    view_terms = lax.map(one_view, jnp.arange(view_count))
    summed = lax.psum_scatter(
        view_terms.transpose(1, 0, 2, 3).astype(jnp.bfloat16),
        "tok",
        scatter_dimension=0,
        tiled=True,
    ).astype(jnp.float32)
    key_grad = summed[:, :, 0].transpose(1, 0, 2).astype(jnp.bfloat16)
    value_grad = summed[:, :, 1].transpose(1, 0, 2).astype(jnp.bfloat16)
    return (attended, query_grad, key_grad, value_grad)


def local(queries, keys, values, grad_out):
    return tokens_layout(queries, keys, values, grad_out)


def solution(mesh):
    return jax.shard_map(
        local,
        mesh=mesh,
        in_specs=(
            P("view", "tok", None),
            P("view", "tok", None),
            P("view", "tok", None),
            P("view", "tok", None),
        ),
        out_specs=(
            P("view", "tok", None),
            P("view", "tok", None),
            P("view", "tok", None),
            P("view", "tok", None),
        ),
        check_vma=False,
    )
```

profile of v0, /device:TPU:0, one launch (start us, length us, event | category | flops | bytes accessed | tf_op | source)
XLA Modules:
  0.0 203.5 jit_solution(9975104969586983579)
XLA Ops:
  7.2 1.1 pad_maximum_fusion.1
  8.4 1.5 copy.92
  9.9 25.9 %all-gather.2.cloned.1.call-done = bf16[2,3,98,1024]{3,0,1,2:T(2,128)(2,1)} async-done(((bf16[2,3,49,1024]{3,0,1,2:T(2,128)(2,1)}), bf16[2,3,98,1024]{3,0,1,2:T(2,128)(2,1)}) %all-gather.2.cloned.1.call-update) | async-done | bytes 1204240 | tf_op jit(solution)/shard_map/all_gather | solution.py:51
  35.8 1.6 copy.93
  37.4 1.1 copy-done.2
  38.6 4.4 %collective-permute-start.1 = (bf16[2,1,98,1024]{3,2,1,0:T(8,128)(2,1)S(1)}, bf16[2,1,98,1024]{3,2,1,0:T(8,128)(2,1)S(1)}, u32[]{:S(2)}, u32[]{:S(2)}) collective-permute-start(bf16[2,1,98,1024]{3,2,1,0:T(8,128)(2,1)S(1)} %get-tuple-element.218), channel_id=1, source_target_pairs={{2,0},{4,2},{6,4},{8,6},{10,8},{12,10},{14,12},{16,14},{18,16},{20... | collective-permute-start | bytes 1204232 | tf_op jit(solution)/shard_map/ppermute | solution.py:19
  43.0 5.9 %collective-permute-done = bf16[2,1,98,1024]{3,2,1,0:T(8,128)(2,1)S(1)} collective-permute-done((bf16[2,1,98,1024]{3,2,1,0:T(8,128)(2,1)S(1)}, bf16[2,1,98,1024]{3,2,1,0:T(8,128)(2,1)S(1)}, u32[]{:S(2)}, u32[]{:S(2)}) %collective-permute-start) | collective-permute-done | bytes 401440 | tf_op jit(solution)/shard_map/ppermute | solution.py:18
  49.3 1.1 slice_bitcast_fusion
  50.5 45.7 %while.24 = (s32[]{:T(128)}, bf16[3,49,1024]{2,1,0:T(8,128)(2,1)}, bf16[3,49,1024]{2,1,0:T(8,128)(2,1)}, f32[3,16,49]{2,1,0:T(8,128)S(1)}, s32[3]{0:T(128)S(1)},...) while((s32[]{:T(128)}, bf16[3,49,1024]{2,1,0:T(8,128)(2,1)}, ...), condition=%wide.region_4.5_spmd, body=%wide.region_0.4_spmd.sunk | while | flops 120668584 | bytes 25146624 | solution.py:80
  50.5 0.7 dynamic_slice.62
  53.2 0.8 reshape.91
  53.9 1.0 copy.140
  55.0 1.1 constant_dynamic-slice_fusion.17
  56.1 0.8 reshape.92
  56.9 1.0 copy.141
  59.9 0.9 constant_dynamic-slice_fusion.19
  62.1 1.5 fusion.60
  63.5 1.1 copy.142
  65.0 0.7 constant_dynamic-update-slice_fusion.8
  65.7 0.7 dynamic_slice.62
  68.4 0.8 reshape.91
  69.2 1.0 copy.140
  70.2 1.1 constant_dynamic-slice_fusion.17
  71.3 0.8 reshape.92
  72.1 1.0 copy.141
  75.1 0.9 constant_dynamic-slice_fusion.19
  77.3 1.5 fusion.60
  78.8 1.1 copy.142
  80.2 0.7 constant_dynamic-update-slice_fusion.8
  81.0 0.7 dynamic_slice.62
  83.6 0.8 reshape.91
  84.4 1.0 copy.140
  85.4 1.1 constant_dynamic-slice_fusion.17
  86.6 0.8 reshape.92
  87.3 1.0 copy.141
  90.3 0.9 constant_dynamic-slice_fusion.19
  92.5 1.5 fusion.60
  94.0 1.1 copy.142
  95.5 0.7 constant_dynamic-update-slice_fusion.8
  96.2 1.2 pad_maximum_fusion.4
  97.4 4.2 %collective-permute-start.3 = (bf16[3,1,49,1024]{3,2,1,0:T(8,128)(2,1)S(1)}, bf16[3,1,49,1024]{3,2,1,0:T(8,128)(2,1)S(1)}, u32[]{:S(2)}, u32[]{:S(2)}) collective-permute-start(bf16[3,1,49,1024]{3,2,1,0:T(8,128)(2,1)S(1)} %get-tuple-element.223), channel_id=1, source_target_pairs={{2,0},{4,2},{6,4},{8,6},{10,8},{12,10},{14,12},{16,14},{18,16},{20... | collective-permute-start | bytes 903176 | tf_op jit(solution)/shard_map/ppermute | solution.py:19
  101.6 4.4 %collective-permute-start.5 = (f32[1,16,49]{2,0,1:T(1,128)S(1)}, f32[1,16,49]{2,0,1:T(1,128)S(1)}, u32[]{:S(2)}, u32[]{:S(2)}) collective-permute-start(f32[1,16,49]{2,0,1:T(1,128)S(1)} %bitcast.123), channel_id=1, source_target_pairs={{2,0},{4,2},{6,4},{8,6},{10,8},{12,10},{14,12},{16,14},{18,16},{20... | collective-permute-start | bytes 9416 | tf_op jit(solution)/shard_map/ppermute | solution.py:19
  106.1 1.2 slice_bitcast_fusion.2
  107.4 4.4 %collective-permute-done.4 = f32[1,16,49]{2,0,1:T(1,128)S(1)} collective-permute-done((f32[1,16,49]{2,0,1:T(1,128)S(1)}, f32[1,16,49]{2,0,1:T(1,128)S(1)}, u32[]{:S(2)}, u32[]{:S(2)}) %collective-permute-start.4) | collective-permute-done | bytes 3168 | tf_op jit(solution)/shard_map/ppermute | solution.py:18
  112.2 1.1 slice_bitcast_fusion.5
  114.7 36.5 %while.25 = (s32[]{:T(128)}, bf16[3,98,2,1024]{3,2,0,1:T(2,128)(2,1)}, s32[3]{0:T(128)S(1)}, bf16[5,49,1024]{2,1,0:T(8,128)(2,1)}, bf16[3,98,1024]{2,1,0:T(8,128...) while((s32[]{:T(128)}, ...), condition=%wide.region_7.8_spmd, body=%wide.region_6.7_spmd.sunk | while | flops 119798344 | bytes 12494044 | solution.py:132
  117.3 1.1 constant_dynamic-slice_fusion.20
  121.6 1.1 constant_dynamic-slice_fusion.21
  122.9 0.8 fusion.68
  124.4 0.9 fusion.70
  125.8 1.1 constant_dynamic-update-slice_fusion.9
  129.4 1.1 constant_dynamic-slice_fusion.20
  133.7 1.1 constant_dynamic-slice_fusion.21
  135.1 0.8 fusion.68
  136.5 0.9 fusion.70
  138.0 1.1 constant_dynamic-update-slice_fusion.9
  141.6 1.1 constant_dynamic-slice_fusion.20
  145.9 1.1 constant_dynamic-slice_fusion.21
  147.3 0.8 fusion.68
  148.7 0.9 fusion.70
  150.2 1.1 constant_dynamic-update-slice_fusion.9
  152.5 40.8 %all-reduce.3.cloned.1.call-done = bf16[98,3,2,1024]{3,2,1,0:T(2,128)(2,1)} async-done(((bf16[98,3,2,1024]{3,2,1,0:T(2,128)(2,1)}), bf16[98,3,2,1024]{3,2,1,0:T(2,128)(2,1)}) %all-reduce.3.cloned.1.call-update) | async-done | bytes 1204240
  193.3 2.3 %constant_dynamic-slice_fusion.9 = (bf16[49,3,1,1024]{3,2,1,0:T(2,128)(2,1)S(1)}, bf16[49,3,1,1024]{3,2,1,0:T(2,128)(2,1)S(1)}) fusion(bf16[98,3,2,1024]{3,2,1,0:T(2,128)(2,1)} %all-reduce.3.cloned.1.call-done, u32[]{:T(128)S(6)} %multiply.1, u32[]{:T(128)S(6)} %convert.2), kind=kLoop, calls=%fused_computation.66 | loop fusion | bytes 1204232 | tf_op jit(solution)/shard_map/slice | solution.py:140
  195.6 1.1 copy_bitcast_fusion
  (133 shorter events, 21.9 us)
Async XLA Ops:
  7.2 28.6 %all-gather.2.cloned.1.call-start = ((), (), s32[]{:S(2)}) async-start(), calls=%async_computation | async-start | bytes 1806336 | tf_op jit(solution)/shard_map/all_gather | solution.py:51
  9.9 183.5 %all-reduce.3.cloned.1.call-start = ((), (), s32[]{:S(2)}) async-start(), calls=%async_computation.1 | async-start | bytes 2408448
  37.4 1.1 copy-start.2
  38.4 10.5 %copy-start.4 = (bf16[2,3,98,1024]{3,0,1,2:T(2,128)(2,1)S(1)}, bf16[2,3,98,1024]{3,0,1,2:T(2,128)(2,1)}, u32[]{:S(2)}) copy-start(bf16[2,3,98,1024]{3,0,1,2:T(2,128)(2,1)} %all-gather.2.cloned.1.call-done) | copy-start | bytes 3612676
  38.5 10.4 %collective-permute-start = (bf16[2,1,98,1024]{3,2,1,0:T(8,128)(2,1)S(1)}, bf16[2,1,98,1024]{3,2,1,0:T(8,128)(2,1)S(1)}, u32[]{:S(2)}, u32[]{:S(2)}) collective-permute-start(bf16[2,1,98,1024]{3,2,1,0:T(8,128)(2,1)S(1)} %get-tuple-element.219), channel_id=1, source_target_pairs={{0,2},{2,4},{4,6},{6,8},{8,10},{10,12},{12,14},{14,16},{16,18},{18... | collective-permute-start | bytes 1204232 | tf_op jit(solution)/shard_map/ppermute | solution.py:18
  38.6 10.7 %collective-permute-start.1 = (bf16[2,1,98,1024]{3,2,1,0:T(8,128)(2,1)S(1)}, bf16[2,1,98,1024]{3,2,1,0:T(8,128)(2,1)S(1)}, u32[]{:S(2)}, u32[]{:S(2)}) collective-permute-start(bf16[2,1,98,1024]{3,2,1,0:T(8,128)(2,1)S(1)} %get-tuple-element.218), channel_id=1, source_target_pairs={{2,0},{4,2},{6,4},{8,6},{10,8},{12,10},{14,12},{16,14},{18,16},{20... | collective-permute-start | bytes 1204232 | tf_op jit(solution)/shard_map/ppermute | solution.py:19
  49.3 1.2 copy-start.5
  50.5 2.6 %copy-start = (bf16[5,98,1024]{2,1,0:T(8,128)(2,1)}, bf16[5,98,1024]{2,1,0:T(8,128)(2,1)S(1)}, u32[]{:S(2)}) copy-start(bf16[5,98,1024]{2,1,0:T(8,128)(2,1)S(1)} %get-tuple-element.399) | copy-start | bytes 3010564 | tf_op jit(solution)/shard_map/while
  63.5 2.2 %copy-start.1 = (bf16[5,98,1024]{2,1,0:T(8,128)(2,1)S(1)}, bf16[5,98,1024]{2,1,0:T(8,128)(2,1)}, u32[]{:S(2)}) copy-start(bf16[5,98,1024]{2,1,0:T(8,128)(2,1)} %copy-done) | copy-start | bytes 3010564 | tf_op jit(solution)/shard_map/while
  63.5 2.2 %copy-start.6 = (bf16[3,49,1024]{2,1,0:T(8,128)(2,1)S(1)}, bf16[3,49,1024]{2,1,0:T(8,128)(2,1)}, u32[]{:S(2)}) copy-start(bf16[3,49,1024]{2,1,0:T(8,128)(2,1)} %get-tuple-element.460) | copy-start | bytes 903172 | tf_op jit(solution)/shard_map/while
  65.7 2.6 %copy-start = (bf16[5,98,1024]{2,1,0:T(8,128)(2,1)}, bf16[5,98,1024]{2,1,0:T(8,128)(2,1)S(1)}, u32[]{:S(2)}) copy-start(bf16[5,98,1024]{2,1,0:T(8,128)(2,1)S(1)} %get-tuple-element.399) | copy-start | bytes 3010564 | tf_op jit(solution)/shard_map/while
  78.8 2.2 %copy-start.1 = (bf16[5,98,1024]{2,1,0:T(8,128)(2,1)S(1)}, bf16[5,98,1024]{2,1,0:T(8,128)(2,1)}, u32[]{:S(2)}) copy-start(bf16[5,98,1024]{2,1,0:T(8,128)(2,1)} %copy-done) | copy-start | bytes 3010564 | tf_op jit(solution)/shard_map/while
  78.8 2.2 %copy-start.6 = (bf16[3,49,1024]{2,1,0:T(8,128)(2,1)S(1)}, bf16[3,49,1024]{2,1,0:T(8,128)(2,1)}, u32[]{:S(2)}) copy-start(bf16[3,49,1024]{2,1,0:T(8,128)(2,1)} %get-tuple-element.460) | copy-start | bytes 903172 | tf_op jit(solution)/shard_map/while
  81.0 2.6 %copy-start = (bf16[5,98,1024]{2,1,0:T(8,128)(2,1)}, bf16[5,98,1024]{2,1,0:T(8,128)(2,1)S(1)}, u32[]{:S(2)}) copy-start(bf16[5,98,1024]{2,1,0:T(8,128)(2,1)S(1)} %get-tuple-element.399) | copy-start | bytes 3010564 | tf_op jit(solution)/shard_map/while
  94.0 2.2 %copy-start.1 = (bf16[5,98,1024]{2,1,0:T(8,128)(2,1)S(1)}, bf16[5,98,1024]{2,1,0:T(8,128)(2,1)}, u32[]{:S(2)}) copy-start(bf16[5,98,1024]{2,1,0:T(8,128)(2,1)} %copy-done) | copy-start | bytes 3010564 | tf_op jit(solution)/shard_map/while
  94.0 2.2 %copy-start.6 = (bf16[3,49,1024]{2,1,0:T(8,128)(2,1)S(1)}, bf16[3,49,1024]{2,1,0:T(8,128)(2,1)}, u32[]{:S(2)}) copy-start(bf16[3,49,1024]{2,1,0:T(8,128)(2,1)} %get-tuple-element.460) | copy-start | bytes 903172 | tf_op jit(solution)/shard_map/while
  96.2 9.9 %copy-start.3 = (bf16[2,3,98,1024]{3,2,1,0:T(8,128)(2,1)S(1)}, bf16[2,3,98,1024]{3,2,1,0:T(8,128)(2,1)}, u32[]{:S(2)}) copy-start(bf16[2,3,98,1024]{3,2,1,0:T(8,128)(2,1)} %copy-done.2) | copy-start | bytes 3612676
  97.4 14.4 %collective-permute-start.3 = (bf16[3,1,49,1024]{3,2,1,0:T(8,128)(2,1)S(1)}, bf16[3,1,49,1024]{3,2,1,0:T(8,128)(2,1)S(1)}, u32[]{:S(2)}, u32[]{:S(2)}) collective-permute-start(bf16[3,1,49,1024]{3,2,1,0:T(8,128)(2,1)S(1)} %get-tuple-element.223), channel_id=1, source_target_pairs={{2,0},{4,2},{6,4},{8,6},{10,8},{12,10},{14,12},{16,14},{18,16},{20... | collective-permute-start | bytes 903176 | tf_op jit(solution)/shard_map/ppermute | solution.py:19
  101.6 10.3 %collective-permute-start.2 = (bf16[3,1,49,1024]{3,2,1,0:T(8,128)(2,1)S(1)}, bf16[3,1,49,1024]{3,2,1,0:T(8,128)(2,1)S(1)}, u32[]{:S(2)}, u32[]{:S(2)}) collective-permute-start(bf16[3,1,49,1024]{3,2,1,0:T(8,128)(2,1)S(1)} %get-tuple-element.222), channel_id=1, source_target_pairs={{0,2},{2,4},{4,6},{6,8},{8,10},{10,12},{12,14},{14,16},{16,18},{18... | collective-permute-start | bytes 903176 | tf_op jit(solution)/shard_map/ppermute | solution.py:18
  101.6 10.3 %copy-start.7 = (bf16[3,49,1024]{2,1,0:T(8,128)(2,1)S(1)}, bf16[3,49,1024]{2,1,0:T(8,128)(2,1)}, u32[]{:S(2)}) copy-start(bf16[3,49,1024]{2,1,0:T(8,128)(2,1)} %get-tuple-element.455) | copy-start | bytes 903172
  101.6 10.3 %copy-start.8 = (bf16[3,49,1024]{2,1,0:T(8,128)(2,1)S(1)}, bf16[3,49,1024]{2,1,0:T(8,128)(2,1)}, u32[]{:S(2)}) copy-start(bf16[3,49,1024]{2,1,0:T(8,128)(2,1)} %get-tuple-element.448) | copy-start | bytes 903172
  101.6 5.8 %collective-permute-start.5 = (f32[1,16,49]{2,0,1:T(1,128)S(1)}, f32[1,16,49]{2,0,1:T(1,128)S(1)}, u32[]{:S(2)}, u32[]{:S(2)}) collective-permute-start(f32[1,16,49]{2,0,1:T(1,128)S(1)} %bitcast.123), channel_id=1, source_target_pairs={{2,0},{4,2},{6,4},{8,6},{10,8},{12,10},{14,12},{16,14},{18,16},{20... | collective-permute-start | bytes 9416 | tf_op jit(solution)/shard_map/ppermute | solution.py:19
  106.0 5.8 %collective-permute-start.4 = (f32[1,16,49]{2,0,1:T(1,128)S(1)}, f32[1,16,49]{2,0,1:T(1,128)S(1)}, u32[]{:S(2)}, u32[]{:S(2)}) collective-permute-start(f32[1,16,49]{2,0,1:T(1,128)S(1)} %bitcast.122), channel_id=1, source_target_pairs={{0,2},{2,4},{4,6},{6,8},{8,10},{10,12},{12,14},{14,16},{16,18},{18... | collective-permute-start | bytes 9416 | tf_op jit(solution)/shard_map/ppermute | solution.py:18
  114.7 36.6 %copy-start.9 = (u32[32]{0:T(128)S(1)}, u32[32]{0:T(128)}, u32[]{:S(2)}) copy-start(u32[32]{0:T(128)} %constant.61) | copy-start | bytes 388
Sparse Core Ops, SparseCore 0:
  10.0 25.7 all-gather.1
  151.4 41.9 all-reduce.2
where the time goes:
time: 204 us
  waiting for transfers between devices  77.2 us (38%)
  local copies, waits for them, and re-layouts  59.2 us (29%)
  loops' own time  20.1 us (10%)
  between operations  14.9 us (7%)
  matrix products  13.6 us (7%)
  starting transfers between devices  13.1 us (6%)
  other arithmetic  5.4 us (3%)
    unnamed x3, waiting for transfers between devices  40.9 us
    all_gather x1, waiting for transfers between devices, tokens_layout(): gathered = lax.all_gather(kv_stack, 'tok', axis=2, tiled=True)  25.9 us
    ppermute x3, starting transfers between devices, padded(): after = lax.ppermute(leading, axis, down)  13 us
    ppermute x3, waiting for transfers between devices, padded(): before = lax.ppermute(last, axis, up)  10.3 us
    another operation x1, loops' own time, tokens_layout(): lax.map(forward_view, jnp.arange(view_count))  10.1 us
    another operation x1, loops' own time, tokens_layout(): view_terms = lax.map(one_view, jnp.arange(view_count))  9.99 us
    reshape x6, local copies, waits for them, and re-layouts, forward_view(): lax.dynamic_slice_in_dim(ext_keys, view_index, 3, 0)  5.34 us
    reshape x6, local copies, waits for them, and re-layouts, forward_view(): lax.dynamic_slice_in_dim(ext_values, view_index, 3, 0)  5.34 us
  transfers between devices with their start and end apart: 8, of which 5 were waited for; matrix products, arithmetic and copies ran while one was open for 1% of the time, Pallas kernels for 0%

commit v1 on v0

v1 whole, which is shorter than its diff:
```python
import functools
import math

import jax
import jax.numpy as jnp
from jax import lax
from jax.experimental import pallas as pl
from jax.experimental.pallas import tpu as pltpu
from jax.sharding import PartitionSpec as P

HEADS = 16
PAD = 64
NEG = -1e30
MESH = pl.DeviceIdType.MESH
F32 = jnp.float32
BF16 = jnp.bfloat16


def kernel(
    groups, parts, q_ref, k_ref, v_ref, g_ref, o_ref, dq_ref, dk_ref, dv_ref,
    qb, gb, kb, vb, ob, dqb, dkb, dvb, hk, hv, rk, rv,
    kp, vp, kt, vt, ak, av,
    in_send, in_recv, own_sem, halo_send, halo_recv, part_send, part_recv, out_send, out_recv,
):
    views, toks, width = q_ref.shape
    lanes = kp.shape[-1]
    half = lanes // 2
    share = width // parts
    chunks = share // lanes
    scale = 1.0 / math.sqrt(half)
    log2e = math.log2(math.e)
    whole8 = toks // 8 * 8
    up8 = (toks + 7) // 8 * 8
    me_v = lax.axis_index("view")
    me_t = lax.axis_index("tok")
    after = lax.rem(me_v + 1, groups)
    before = lax.rem(me_v + groups - 1, groups)
    peers = [lax.rem(me_t + s, parts) for s in range(parts)]

    barrier = pltpu.get_barrier_semaphore()
    for dev in [(before, me_t), (after, me_t)] + [(me_v, p) for p in peers[1:]]:
        pl.semaphore_signal(barrier, inc=1, device_id=dev, device_id_type=MESH)
    pl.semaphore_wait(barrier, parts + 1)

    def span(owner, c):
        return pl.ds(pl.multiple_of(owner * share + c * lanes, lanes), lanes)

    ins = (q_ref, g_ref, k_ref, v_ref)

    def landing(a, c, s):
        if a < 2:
            return (qb, gb)[a].at[c, s]
        return (kb, vb)[a - 2].at[c, s, pl.ds(1, views)]

    def in_copy(a, c, s):
        return pltpu.make_async_remote_copy(
            src_ref=ins[a].at[:, :, span(peers[s], c)],
            dst_ref=landing(a, c, parts - s),
            send_sem=in_send.at[c, s, a],
            recv_sem=in_recv.at[c, parts - s, a],
            device_id=(me_v, peers[s]),
            device_id_type=MESH,
        )

    def own_copy(a, c):
        return pltpu.make_async_copy(
            ins[a].at[:, :, span(me_t, c)], landing(a, c, 0), own_sem.at[c, a]
        )

    def halo_copy(a, c, s, way):
        buf = (kb, vb)[a]
        src, dst, dev = ((1, views + 1, before), (views, 0, after))[way]
        return pltpu.make_async_remote_copy(
            src_ref=buf.at[c, s, src],
            dst_ref=buf.at[c, s, dst],
            send_sem=halo_send.at[c, s, a, way],
            recv_sem=halo_recv.at[c, s, a, way],
            device_id=(dev, me_t),
            device_id_type=MESH,
        )

    def part_copy(a, c, way):
        return pltpu.make_async_remote_copy(
            src_ref=(hk, hv)[a].at[c, way],
            dst_ref=(rk, rv)[a].at[c, way],
            send_sem=part_send.at[c, a, way],
            recv_sem=part_recv.at[c, a, way],
            device_id=((before, after)[way], me_t),
            device_id_type=MESH,
        )

    outs = (o_ref, dq_ref, dk_ref, dv_ref)

    def out_copy(a, c, s):
        return pltpu.make_async_remote_copy(
            src_ref=(ob, dqb, dkb, dvb)[a].at[c, s],
            dst_ref=outs[a].at[:, :, span(me_t, c)],
            send_sem=out_send.at[c, s, a],
            recv_sem=out_recv.at[c, parts - s, a],
            device_id=(me_v, peers[s]),
            device_id_type=MESH,
        )

    def out_arrival(a, c, s):
        return pltpu.make_async_remote_copy(
            src_ref=(ob, dqb, dkb, dvb)[a].at[c, s],
            dst_ref=outs[a].at[:, :, span(peers[s], c)],
            send_sem=out_send.at[c, s, a],
            recv_sem=out_recv.at[c, s, a],
            device_id=(me_v, peers[s]),
            device_id_type=MESH,
        )

    @pl.loop(0, chunks)
    def _(c):
        for s in range(1, parts):
            for a in (2, 3, 0, 1):
                in_copy(a, c, s).start()
        for a in (2, 3, 0, 1):
            own_copy(a, c).start()

    def pad(x):
        return jnp.concatenate([x, jnp.zeros((PAD - toks, lanes), x.dtype)], axis=0)

    def stage(c, w):
        for buf, rows, cols in ((kb, kp, kt), (vb, vp, vt)):
            block = jnp.concatenate([pad(buf[c, s, w]) for s in range(parts)], axis=0)
            rows[w] = block
            cols[w] = block.T

    lane = lax.broadcasted_iota(jnp.int32, (2 * PAD, lanes), 1)
    row_ok = lax.broadcasted_iota(jnp.int32, (up8 - whole8, 2 * lanes), 0) < toks - whole8
    blocks = 3 * parts

    def twin(x):
        zero = jnp.zeros_like(x)
        return jnp.concatenate([jnp.where(lane < half, x, zero), jnp.where(lane < half, zero, x)], 0)

    def full(x):
        filler = jnp.zeros((blocks, PAD - up8, 2 * lanes), F32)
        return jnp.concatenate([x, filler], axis=1).reshape(blocks * PAD, 2 * lanes).astype(BF16)

    def diagonal(x):
        return jnp.concatenate([x[:half, :lanes], x[half:, lanes:]], axis=0).T

    def dot(x, y):
        return jnp.dot(x, y, preferred_element_type=F32)

    def dot_t(x, y):
        return lax.dot_general(x, y, (((1,), (1,)), ((), ())), preferred_element_type=F32)

    def compute(c, v):
        key_rows = kp[v : v + 3].reshape(blocks * PAD, lanes)
        value_rows = vp[v : v + 3].reshape(blocks * PAD, lanes)
        key_cols = jnp.concatenate([kt[v + j] for j in range(3)], axis=1)
        value_cols = jnp.concatenate([vt[v + j] for j in range(3)], axis=1)
        for s in range(0, parts, 2):
            query = jnp.concatenate([pad(qb[c, s + i, v]) for i in range(2)], axis=0)
            grad = jnp.concatenate([pad(gb[c, s + i, v]) for i in range(2)], axis=0)
            query = twin(query * jnp.asarray(scale, BF16))
            grad = twin(grad)
            scores = dot_t(key_rows, query).reshape(blocks, PAD, 2 * lanes)
            tail = jnp.where(row_ok[None], scores[:, whole8:up8], NEG)
            scores = jnp.concatenate([scores[:, :whole8], tail], axis=1)
            top = jnp.max(scores, axis=(0, 1), keepdims=True)
            probs = jnp.exp2((scores - top) * log2e)
            probs = probs * (1.0 / jnp.sum(probs, axis=(0, 1), keepdims=True))
            grad_probs = dot_t(value_rows, grad).reshape(blocks, PAD, 2 * lanes)[:, :up8]
            weighted = probs * grad_probs
            delta = jnp.sum(weighted, axis=(0, 1), keepdims=True)
            probs_bf = full(probs)
            grad_bf = full(weighted - probs * delta)
            key_term = dot(grad_bf, query).reshape(3, parts * PAD, lanes)
            value_term = dot(probs_bf, grad).reshape(3, parts * PAD, lanes)
            ak[v : v + 3] += key_term
            av[v : v + 3] += value_term
            attended = diagonal(dot(value_cols, probs_bf)).astype(BF16)
            query_grad = (diagonal(dot(key_cols, grad_bf)) * scale).astype(BF16)
            for i in range(2):
                rows = slice(i * PAD, i * PAD + toks)
                if s + i == 0:
                    o_ref[v, :, span(me_t, c)] = attended[rows]
                    dq_ref[v, :, span(me_t, c)] = query_grad[rows]
                else:
                    ob[c, s + i, v] = attended[rows]
                    dqb[c, s + i, v] = query_grad[rows]

    def finish(c, sums_k, sums_v):
        for a, (sums, buf, ref, got) in enumerate(
            ((sums_k, dkb, dk_ref, rk), (sums_v, dvb, dv_ref, rv))
        ):
            part_copy(a, c, 0).wait_recv()
            part_copy(a, c, 1).wait_recv()
            for s in range(parts):
                for v in range(views):
                    total = sums[v + 1, s * PAD : s * PAD + toks]
                    if v == 0:
                        total = total + got[c, 1, s].astype(F32)
                    if v == views - 1:
                        total = total + got[c, 0, s].astype(F32)
                    if s == 0:
                        ref[v, :, span(me_t, c)] = total.astype(BF16)
                    else:
                        buf[c, s, v] = total.astype(BF16)
            for s in range(1, parts):
                out_copy(2 + a, c, s).start()

    @pl.loop(0, chunks)
    def _(c):
        for a in (2, 3):
            own_copy(a, c).wait()
        for a in range(2):
            for way in range(2):
                halo_copy(a, c, 0, way).start()
        for s in range(1, parts):
            for a in (2, 3):
                in_copy(a, c, parts - s).wait_recv()
            for a in range(2):
                for way in range(2):
                    halo_copy(a, c, s, way).start()
        for w in range(1, views + 1):
            stage(c, w)
        ak[...] = jnp.zeros_like(ak)
        av[...] = jnp.zeros_like(av)
        for a in (0, 1):
            own_copy(a, c).wait()
            for s in range(1, parts):
                in_copy(a, c, parts - s).wait_recv()
        for v in range(1, views - 1):
            compute(c, v)
        for s in range(parts):
            for a in range(2):
                for way in range(2):
                    halo_copy(a, c, s, way).wait_recv()
        stage(c, 0)
        stage(c, views + 1)
        compute(c, 0)
        if views > 1:
            compute(c, views - 1)
        for a, (sums, edge) in enumerate(((ak, hk), (av, hv))):
            for way, w in enumerate((0, views + 1)):
                for s in range(parts):
                    edge[c, way, s] = sums[w, s * PAD : s * PAD + toks].astype(BF16)
                part_copy(a, c, way).start()
        for a in range(2):
            for s in range(1, parts):
                out_copy(a, c, s).start()
        finish(c, ak, av)

    @pl.loop(0, chunks)
    def _(c):
        for a in range(4):
            for s in range(1, parts):
                in_copy(a, c, s).wait_send()
                out_copy(a, c, s).wait_send()
                out_arrival(a, c, s).wait_recv()
        for a in range(2):
            for way in range(2):
                part_copy(a, c, way).wait_send()
                for s in range(parts):
                    halo_copy(a, c, s, way).wait_send()


def solution(mesh):
    groups, parts = mesh.shape["view"], mesh.shape["tok"]

    def local(queries, keys, values, grad_out):
        views, toks, width = queries.shape
        lanes = 2 * (width // HEADS)
        chunks = width // parts // lanes
        vmem = pltpu.VMEM
        dma = pltpu.SemaphoreType.DMA
        part = vmem((chunks, parts, views, toks, lanes), BF16)
        wide = vmem((chunks, parts, views + 2, toks, lanes), BF16)
        edge = vmem((chunks, 2, parts, toks, lanes), BF16)
        rows = vmem((views + 2, parts * PAD, lanes), BF16)
        cols = vmem((views + 2, lanes, parts * PAD), BF16)
        sums = vmem((views + 2, parts * PAD, lanes), F32)
        shape = jax.ShapeDtypeStruct(queries.shape, BF16)
        flops = 12 * views * parts * toks * 3 * parts * toks * (width // parts)
        return pl.pallas_call(
            functools.partial(kernel, groups, parts),
            out_shape=(shape,) * 4,
            in_specs=[pl.BlockSpec(memory_space=pltpu.VMEM)] * 4,
            out_specs=[pl.BlockSpec(memory_space=pltpu.VMEM)] * 4,
            scratch_shapes=[
                part, part, wide, wide, part, part, part, part, edge, edge, edge, edge,
                rows, rows, cols, cols, sums, sums,
                dma((chunks, parts, 4)), dma((chunks, parts, 4)), dma((chunks, 4)),
                dma((chunks, parts, 2, 2)), dma((chunks, parts, 2, 2)),
                dma((chunks, 2, 2)), dma((chunks, 2, 2)),
                dma((chunks, parts, 4)), dma((chunks, parts, 4)),
            ],
            cost_estimate=pl.CostEstimate(
                flops=flops, bytes_accessed=16 * views * toks * width, transcendentals=0
            ),
            compiler_params=pltpu.CompilerParams(
                collective_id=0, has_side_effects=True, vmem_limit_bytes=48 * 1024 * 1024
            ),
        )(queries, keys, values, grad_out)

    spec = P("view", "tok", None)
    return jax.shard_map(
        local, mesh=mesh, in_specs=(spec,) * 4, out_specs=(spec,) * 4, check_vma=False
    )
```

time: 204 us -> 61 us (0.30)
  waiting for transfers between devices: 77.2 us -> 0 us
  Pallas kernels: 0 us -> 53.2 us
  local copies, waits for them, and re-layouts: 59.2 us -> 6.83 us
  loops' own time: 20.1 us -> 0 us
  between operations: 14.9 us -> 0.65 us
  matrix products: 13.6 us -> 0 us
  starting transfers between devices: 13.1 us -> 0 us
  other arithmetic: 5.4 us -> 0 us
    pallas_call x0 -> x1, Pallas kernels: none -> 53.2 us  [local(): pl.pallas_call(functools.partial(kernel, groups, parts), out_shape=(shape...]
    unnamed x3 -> x0, waiting for transfers between devices: 40.9 us -> none
    all_gather x1 -> x0, waiting for transfers between devices: 25.9 us -> none  [tokens_layout(): gathered = lax.all_gather(kv_stack, 'tok', axis=2, tiled=True)]
    another operation x2 -> x0, loops' own time: 20.1 us -> none  [the longest x1 10.1 us: tokens_layout(): lax.map(forward_view, jnp.arange(view_count))]
    dynamic_slice x30 -> x0, local copies, waits for them, and re-layouts: 17.7 us -> none  [the longest x6 3.74 us: tokens_layout(): lax.map(forward_view, jnp.arange(view_count))]
    reshape x30 -> x0, local copies, waits for them, and re-layouts: 17.3 us -> none  [the longest x6 5.34 us: forward_view(): lax.dynamic_slice_in_dim(ext_keys, view_index, 3, 0)]
    dot_general x18 -> x0, matrix products: 13.6 us -> none  [the longest x3 4.41 us: attend_view(): jnp.einsum('hqk,khd->qhd', grad_bf, key_window, preferred_element_type=f32)]
    ppermute x6 -> x0, starting transfers between devices: 13 us -> none  [the longest x3 13 us: padded(): after = lax.ppermute(leading, axis, down)]
  transfers between devices with their start and end apart: 8 -> 0, of which waited for: 5 -> 0; matrix products, arithmetic and copies ran while one was open for 1% -> 0% of each run, Pallas kernels for 0% -> 0%
where the time goes in v1:
time: 61 us; the launch traced here: 60.7 us
  Pallas kernels  53.2 us (87%)
  local copies, waits for them, and re-layouts  6.83 us (11%)
  between operations  0.65 us (1%)
    pallas_call x1, Pallas kernels, local(): pl.pallas_call(functools.partial(kernel, groups, parts), out_shape=(shape...  53.2 us
    unnamed x12, local copies, waits for them, and re-layouts  6.83 us

profile of v1, /device:TPU:0, one launch (start us, length us, event | category | flops | bytes accessed | tf_op | source)
XLA Modules:
  0.0 60.7 jit_solution(11814599817900631338)
XLA Ops:
  0.6 0.0 copy-start
  0.6 1.0 %copy-done = bf16[3,49,1024]{2,1,0:T(8,128)(2,1)S(1)} copy-done((bf16[3,49,1024]{2,1,0:T(8,128)(2,1)S(1)}, bf16[3,49,1024]{2,1,0:T(8,128)(2,1)}, u32[]{:S(2)}) %copy-start) | copy-done | bytes 301080
  1.6 0.0 copy-start.1
  1.6 1.0 %copy-done.1 = bf16[3,49,1024]{2,1,0:T(8,128)(2,1)S(1)} copy-done((bf16[3,49,1024]{2,1,0:T(8,128)(2,1)S(1)}, bf16[3,49,1024]{2,1,0:T(8,128)(2,1)}, u32[]{:S(2)}) %copy-start.1) | copy-done | bytes 301080
  2.6 0.0 copy-start.2
  2.6 1.0 %copy-done.2 = bf16[3,49,1024]{2,1,0:T(8,128)(2,1)S(1)} copy-done((bf16[3,49,1024]{2,1,0:T(8,128)(2,1)S(1)}, bf16[3,49,1024]{2,1,0:T(8,128)(2,1)}, u32[]{:S(2)}) %copy-start.2) | copy-done | bytes 301080
  3.6 0.0 copy-start.3
  3.6 1.0 %copy-done.3 = bf16[3,49,1024]{2,1,0:T(8,128)(2,1)S(1)} copy-done((bf16[3,49,1024]{2,1,0:T(8,128)(2,1)S(1)}, bf16[3,49,1024]{2,1,0:T(8,128)(2,1)}, u32[]{:S(2)}) %copy-start.3) | copy-done | bytes 301080
  4.5 53.2 %shard_map.75 = (bf16[3,49,1024]{2,1,0:T(8,128)(2,1)S(1)}, bf16[3,49,1024]{2,1,0:T(8,128)(2,1)S(1)}, bf16[3,49,1024]{2,1,0:T(8,128)(2,1)S(1)}, bf16[3,49,1024]{2,1,0:T(8,128)(2,1)S(1)}) custom-call(bf16[3,49,1024]{2,1,0:T(8,128)(2,1)S(1)} %copy-done, bf16[3,49,1024]{2,1,0:T(8,128)(2,1)S(1)} %copy-done.1, bf16[3,49,1024]{2,1,0:T(8,128)(2,1)S(1)} %copy-done.2, ...), custom_call_target="tpu_custom_call" | custom-call | flops 531062784 | bytes 2408448 | tf_op jit(solution)/shard_map/pallas_call | solution.py:281
  57.8 0.7 %copy.12 = bf16[3,49,1024]{2,1,0:T(8,128)(2,1)} copy(bf16[3,49,1024]{2,1,0:T(8,128)(2,1)S(1)} %get-tuple-element.8) | data formatting | bytes 602112
  58.5 0.7 %copy.13 = bf16[3,49,1024]{2,1,0:T(8,128)(2,1)} copy(bf16[3,49,1024]{2,1,0:T(8,128)(2,1)S(1)} %get-tuple-element.9) | data formatting | bytes 602112
  59.2 0.7 %copy.14 = bf16[3,49,1024]{2,1,0:T(8,128)(2,1)} copy(bf16[3,49,1024]{2,1,0:T(8,128)(2,1)S(1)} %get-tuple-element.10) | data formatting | bytes 602112
  60.0 0.7 %copy.15 = bf16[3,49,1024]{2,1,0:T(8,128)(2,1)} copy(bf16[3,49,1024]{2,1,0:T(8,128)(2,1)S(1)} %get-tuple-element.11) | data formatting | bytes 602112
Async XLA Ops:
  0.6 1.0 %copy-start = (bf16[3,49,1024]{2,1,0:T(8,128)(2,1)S(1)}, bf16[3,49,1024]{2,1,0:T(8,128)(2,1)}, u32[]{:S(2)}) copy-start(bf16[3,49,1024]{2,1,0:T(8,128)(2,1)} %q_ref.1) | copy-start | bytes 903172
  1.6 1.0 %copy-start.1 = (bf16[3,49,1024]{2,1,0:T(8,128)(2,1)S(1)}, bf16[3,49,1024]{2,1,0:T(8,128)(2,1)}, u32[]{:S(2)}) copy-start(bf16[3,49,1024]{2,1,0:T(8,128)(2,1)} %k_ref.1) | copy-start | bytes 903172
  2.6 1.0 %copy-start.2 = (bf16[3,49,1024]{2,1,0:T(8,128)(2,1)S(1)}, bf16[3,49,1024]{2,1,0:T(8,128)(2,1)}, u32[]{:S(2)}) copy-start(bf16[3,49,1024]{2,1,0:T(8,128)(2,1)} %v_ref.1) | copy-start | bytes 903172
  3.6 1.0 %copy-start.3 = (bf16[3,49,1024]{2,1,0:T(8,128)(2,1)S(1)}, bf16[3,49,1024]{2,1,0:T(8,128)(2,1)}, u32[]{:S(2)}) copy-start(bf16[3,49,1024]{2,1,0:T(8,128)(2,1)} %g_ref.1) | copy-start | bytes 903172

commit v2 on v1

--- a/solution.py
+++ b/solution.py
@@ -18,7 +18,7 @@
 
 def kernel(
     groups, parts, q_ref, k_ref, v_ref, g_ref, o_ref, dq_ref, dk_ref, dv_ref,
-    qb, gb, kb, vb, ob, dqb, dkb, dvb, hk, hv, rk, rv,
+    qb, gb, kvb, ob, dqb, dkb, dvb, edge, got,
     kp, vp, kt, vt, ak, av,
     in_send, in_recv, own_sem, halo_send, halo_recv, part_send, part_recv, out_send, out_recv,
 ):
@@ -50,7 +50,7 @@
     def landing(a, c, s):
         if a < 2:
             return (qb, gb)[a].at[c, s]
-        return (kb, vb)[a - 2].at[c, s, pl.ds(1, views)]
+        return kvb.at[c, pl.ds(1, views), s, a - 2]
 
     def in_copy(a, c, s):
         return pltpu.make_async_remote_copy(
@@ -67,24 +67,24 @@
             ins[a].at[:, :, span(me_t, c)], landing(a, c, 0), own_sem.at[c, a]
         )
 
-    def halo_copy(a, c, s, way):
-        buf = (kb, vb)[a]
+    def halo_copy(c, late, way):
+        slots = pl.ds(1, parts - 1) if late else pl.ds(0, 1)
         src, dst, dev = ((1, views + 1, before), (views, 0, after))[way]
         return pltpu.make_async_remote_copy(
-            src_ref=buf.at[c, s, src],
-            dst_ref=buf.at[c, s, dst],
-            send_sem=halo_send.at[c, s, a, way],
-            recv_sem=halo_recv.at[c, s, a, way],
+            src_ref=kvb.at[c, src, slots],
+            dst_ref=kvb.at[c, dst, slots],
+            send_sem=halo_send.at[c, late, way],
+            recv_sem=halo_recv.at[c, late, way],
             device_id=(dev, me_t),
             device_id_type=MESH,
         )
 
-    def part_copy(a, c, way):
-        return pltpu.make_async_remote_copy(
-            src_ref=(hk, hv)[a].at[c, way],
-            dst_ref=(rk, rv)[a].at[c, way],
-            send_sem=part_send.at[c, a, way],
-            recv_sem=part_recv.at[c, a, way],
+    def part_copy(c, way):
+        return pltpu.make_async_remote_copy(
+            src_ref=edge.at[c, way],
+            dst_ref=got.at[c, way],
+            send_sem=part_send.at[c, way],
+            recv_sem=part_recv.at[c, way],
             device_id=((before, after)[way], me_t),
             device_id_type=MESH,
         )
@@ -111,22 +111,69 @@
             device_id_type=MESH,
         )
 
+    def send_in(pair, c):
+        for s in range(1, parts):
+            for a in pair:
+                in_copy(a, c, s).start()
+
+    for a in (2, 3):
+        own_copy(a, 0).start()
+    send_in((2, 3), 0)
+    for a in (0, 1):
+        own_copy(a, 0).start()
+    send_in((0, 1), 0)
+    if chunks > 1:
+        send_in((2, 3), 1)
+
+    @pl.loop(1, chunks)
+    def _(c):
+        @pl.when(c + 1 < chunks)
+        def _():
+            send_in((2, 3), c + 1)
+
+        send_in((0, 1), c)
+        for a in (2, 3, 0, 1):
+            own_copy(a, c).start()
+
     @pl.loop(0, chunks)
     def _(c):
+        for a in (2, 3):
+            own_copy(a, c).wait()
+        for way in range(2):
+            halo_copy(c, 0, way).start()
+
+    def relay(c):
         for s in range(1, parts):
-            for a in (2, 3, 0, 1):
-                in_copy(a, c, s).start()
-        for a in (2, 3, 0, 1):
-            own_copy(a, c).start()
+            for a in (2, 3):
+                in_copy(a, c, parts - s).wait_recv()
+        for way in range(2):
+            halo_copy(c, 1, way).start()
+
+    def queries_ready(c):
+        for a in (0, 1):
+            own_copy(a, c).wait()
+            for s in range(1, parts):
+                in_copy(a, c, parts - s).wait_recv()
 
     def pad(x):
         return jnp.concatenate([x, jnp.zeros((PAD - toks, lanes), x.dtype)], axis=0)
 
     def stage(c, w):
-        for buf, rows, cols in ((kb, kp, kt), (vb, vp, vt)):
-            block = jnp.concatenate([pad(buf[c, s, w]) for s in range(parts)], axis=0)
+        for a, rows, cols in ((0, kp, kt), (1, vp, vt)):
+            block = jnp.concatenate([pad(kvb[c, w, s, a]) for s in range(parts)], axis=0)
             rows[w] = block
             cols[w] = block.T
+
+    def stage_own(c):
+        for w in range(1, views + 1):
+            stage(c, w)
+
+    def stage_halo(c):
+        for late in range(2):
+            for way in range(2):
+                halo_copy(c, late, way).wait_recv()
+        stage(c, 0)
+        stage(c, views + 1)
 
     lane = lax.broadcasted_iota(jnp.int32, (2 * PAD, lanes), 1)
     row_ok = lax.broadcasted_iota(jnp.int32, (up8 - whole8, 2 * lanes), 0) < toks - whole8
@@ -150,6 +197,7 @@
         return lax.dot_general(x, y, (((1,), (1,)), ((), ())), preferred_element_type=F32)
 
     def compute(c, v):
+        now = lax.rem(c, 2)
         key_rows = kp[v : v + 3].reshape(blocks * PAD, lanes)
         value_rows = vp[v : v + 3].reshape(blocks * PAD, lanes)
         key_cols = jnp.concatenate([kt[v + j] for j in range(3)], axis=1)
@@ -172,8 +220,8 @@
             grad_bf = full(weighted - probs * delta)
             key_term = dot(grad_bf, query).reshape(3, parts * PAD, lanes)
             value_term = dot(probs_bf, grad).reshape(3, parts * PAD, lanes)
-            ak[v : v + 3] += key_term
-            av[v : v + 3] += value_term
+            ak[now, v : v + 3] += key_term
+            av[now, v : v + 3] += value_term
             attended = diagonal(dot(value_cols, probs_bf)).astype(BF16)
             query_grad = (diagonal(dot(key_cols, grad_bf)) * scale).astype(BF16)
             for i in range(2):
@@ -185,67 +233,78 @@
                     ob[c, s + i, v] = attended[rows]
                     dqb[c, s + i, v] = query_grad[rows]
 
-    def finish(c, sums_k, sums_v):
-        for a, (sums, buf, ref, got) in enumerate(
-            ((sums_k, dkb, dk_ref, rk), (sums_v, dvb, dv_ref, rv))
-        ):
-            part_copy(a, c, 0).wait_recv()
-            part_copy(a, c, 1).wait_recv()
-            for s in range(parts):
+    def clear(c):
+        now = lax.rem(c, 2)
+        ak[now] = jnp.zeros(ak.shape[1:], F32)
+        av[now] = jnp.zeros(av.shape[1:], F32)
+
+    def middle(c):
+        for v in range(1, views - 1):
+            compute(c, v)
+
+    def edges(c):
+        compute(c, 0)
+        if views > 1:
+            compute(c, views - 1)
+        now = lax.rem(c, 2)
+        for way, w in enumerate((0, views + 1)):
+            for a, sums in enumerate((ak, av)):
+                for s in range(parts):
+                    edge[c, way, a, s] = sums[now, w, s * PAD : s * PAD + toks].astype(BF16)
+            part_copy(c, way).start()
+
+    def send_rows(c):
+        for s in range(1, parts):
+            for a in range(2):
+                out_copy(a, c, s).start()
+
+    def finish(c):
+        now = lax.rem(c, 2)
+        for way in range(2):
+            part_copy(c, way).wait_recv()
+        for a, (sums, buf, ref) in enumerate(((ak, dkb, dk_ref), (av, dvb, dv_ref))):
+            for s in reversed(range(parts)):
                 for v in range(views):
-                    total = sums[v + 1, s * PAD : s * PAD + toks]
+                    total = sums[now, v + 1, s * PAD : s * PAD + toks]
                     if v == 0:
-                        total = total + got[c, 1, s].astype(F32)
+                        total = total + got[c, 1, a, s].astype(F32)
                     if v == views - 1:
-                        total = total + got[c, 0, s].astype(F32)
+                        total = total + got[c, 0, a, s].astype(F32)
                     if s == 0:
                         ref[v, :, span(me_t, c)] = total.astype(BF16)
                     else:
                         buf[c, s, v] = total.astype(BF16)
-            for s in range(1, parts):
-                out_copy(2 + a, c, s).start()
-
-    @pl.loop(0, chunks)
+                if s > 0:
+                    out_copy(2 + a, c, s).start()
+
+    relay(0)
+    stage_own(0)
+    clear(0)
+    queries_ready(0)
+    middle(0)
+    if chunks > 1:
+        relay(1)
+    stage_halo(0)
+    edges(0)
+    send_rows(0)
+
+    @pl.loop(1, chunks)
     def _(c):
-        for a in (2, 3):
-            own_copy(a, c).wait()
-        for a in range(2):
-            for way in range(2):
-                halo_copy(a, c, 0, way).start()
-        for s in range(1, parts):
-            for a in (2, 3):
-                in_copy(a, c, parts - s).wait_recv()
-            for a in range(2):
-                for way in range(2):
-                    halo_copy(a, c, s, way).start()
-        for w in range(1, views + 1):
-            stage(c, w)
-        ak[...] = jnp.zeros_like(ak)
-        av[...] = jnp.zeros_like(av)
-        for a in (0, 1):
-            own_copy(a, c).wait()
-            for s in range(1, parts):
-                in_copy(a, c, parts - s).wait_recv()
-        for v in range(1, views - 1):
-            compute(c, v)
-        for s in range(parts):
-            for a in range(2):
-                for way in range(2):
-                    halo_copy(a, c, s, way).wait_recv()
-        stage(c, 0)
-        stage(c, views + 1)
-        compute(c, 0)
-        if views > 1:
-            compute(c, views - 1)
-        for a, (sums, edge) in enumerate(((ak, hk), (av, hv))):
-            for way, w in enumerate((0, views + 1)):
-                for s in range(parts):
-                    edge[c, way, s] = sums[w, s * PAD : s * PAD + toks].astype(BF16)
-                part_copy(a, c, way).start()
-        for a in range(2):
-            for s in range(1, parts):
-                out_copy(a, c, s).start()
-        finish(c, ak, av)
+        stage_own(c)
+        clear(c)
+
+        @pl.when(c + 1 < chunks)
+        def _():
+            relay(c + 1)
+
+        queries_ready(c)
+        stage_halo(c)
+        edges(c)
+        finish(c - 1)
+        middle(c)
+        send_rows(c)
+
+    finish(chunks - 1)
 
     @pl.loop(0, chunks)
     def _(c):
@@ -254,11 +313,21 @@
                 in_copy(a, c, s).wait_send()
                 out_copy(a, c, s).wait_send()
                 out_arrival(a, c, s).wait_recv()
-        for a in range(2):
-            for way in range(2):
-                part_copy(a, c, way).wait_send()
-                for s in range(parts):
-                    halo_copy(a, c, s, way).wait_send()
+        for way in range(2):
+            part_copy(c, way).wait_send()
+            for late in range(2):
+                halo_copy(c, late, way).wait_send()
+
+
+def deliver(*refs):
+    count = len(refs) // 2
+    copies = [
+        pltpu.make_async_copy(refs[i], refs[count + i], refs[-1].at[i]) for i in range(count)
+    ]
+    for copy in copies:
+        copy.start()
+    for copy in copies:
+        copy.wait()
 
 
 def solution(mesh):
@@ -271,33 +340,41 @@
         vmem = pltpu.VMEM
         dma = pltpu.SemaphoreType.DMA
         part = vmem((chunks, parts, views, toks, lanes), BF16)
-        wide = vmem((chunks, parts, views + 2, toks, lanes), BF16)
-        edge = vmem((chunks, 2, parts, toks, lanes), BF16)
+        pairs = vmem((chunks, views + 2, parts, 2, toks, lanes), BF16)
+        edge = vmem((chunks, 2, 2, parts, toks, lanes), BF16)
         rows = vmem((views + 2, parts * PAD, lanes), BF16)
         cols = vmem((views + 2, lanes, parts * PAD), BF16)
-        sums = vmem((views + 2, parts * PAD, lanes), F32)
+        sums = vmem((2, views + 2, parts * PAD, lanes), F32)
         shape = jax.ShapeDtypeStruct(queries.shape, BF16)
         flops = 12 * views * parts * toks * 3 * parts * toks * (width // parts)
-        return pl.pallas_call(
+        results = pl.pallas_call(
             functools.partial(kernel, groups, parts),
             out_shape=(shape,) * 4,
-            in_specs=[pl.BlockSpec(memory_space=pltpu.VMEM)] * 4,
+            in_specs=[pl.BlockSpec(memory_space=pl.ANY)] * 4,
             out_specs=[pl.BlockSpec(memory_space=pltpu.VMEM)] * 4,
             scratch_shapes=[
-                part, part, wide, wide, part, part, part, part, edge, edge, edge, edge,
+                part, part, pairs, part, part, part, part, edge, edge,
                 rows, rows, cols, cols, sums, sums,
                 dma((chunks, parts, 4)), dma((chunks, parts, 4)), dma((chunks, 4)),
-                dma((chunks, parts, 2, 2)), dma((chunks, parts, 2, 2)),
                 dma((chunks, 2, 2)), dma((chunks, 2, 2)),
+                dma((chunks, 2)), dma((chunks, 2)),
                 dma((chunks, parts, 4)), dma((chunks, parts, 4)),
             ],
             cost_estimate=pl.CostEstimate(
                 flops=flops, bytes_accessed=16 * views * toks * width, transcendentals=0
             ),
             compiler_params=pltpu.CompilerParams(
-                collective_id=0, has_side_effects=True, vmem_limit_bytes=48 * 1024 * 1024
+                collective_id=0, has_side_effects=True, vmem_limit_bytes=58 * 1024 * 1024
             ),
         )(queries, keys, values, grad_out)
+        return pl.pallas_call(
+            deliver,
+            out_shape=(shape,) * 4,
+            in_specs=[pl.BlockSpec(memory_space=pl.ANY)] * 4,
+            out_specs=[pl.BlockSpec(memory_space=pl.ANY)] * 4,
+            scratch_shapes=[dma((4,))],
+            compiler_params=pltpu.CompilerParams(vmem_limit_bytes=58 * 1024 * 1024),
+        )(*results)
 
     spec = P("view", "tok", None)
     return jax.shard_map(

time: 61 us -> 81.7 us (1.34)
  Pallas kernels: 53.2 us -> 80.8 us
  local copies, waits for them, and re-layouts: 6.83 us -> 0 us
    pallas_call x0 -> x1, Pallas kernels: none -> 42.8 us  [local(): pl.pallas_call(deliver, out_shape=(shape,) * 4, in_specs=[pl.BlockSpec(me...]
    pallas_call x1, Pallas kernels: 53.2 us -> 38 us  [local(): pl.pallas_call(functools.partial(kernel, groups, parts), out_shape=(shape...]
    unnamed x12 -> x0, local copies, waits for them, and re-layouts: 6.83 us -> none
where the time goes in v2:
time: 81.7 us; the launch traced here: 81.5 us
  Pallas kernels  80.8 us (99%)
    pallas_call x1, Pallas kernels, local(): pl.pallas_call(deliver, out_shape=(shape,) * 4, in_specs=[pl.BlockSpec(me...  42.8 us
    pallas_call x1, Pallas kernels, local(): pl.pallas_call(functools.partial(kernel, groups, parts), out_shape=(shape...  38 us

profile of v2, /device:TPU:0, one launch (start us, length us, event | category | flops | bytes accessed | tf_op | source)
XLA Modules:
  0.0 81.5 jit_solution(9873180463777728013)
XLA Ops:
  0.6 38.0 %shard_map.75 = (bf16[3,49,1024]{2,1,0:T(8,128)(2,1)}, bf16[3,49,1024]{2,1,0:T(8,128)(2,1)}, bf16[3,49,1024]{2,1,0:T(8,128)(2,1)}, bf16[3,49,1024]{2,1,0:T(8,128)(2,1)}) custom-call(bf16[3,49,1024]{2,1,0:T(8,128)(2,1)} %q_ref.1, bf16[3,49,1024]{2,1,0:T(8,128)(2,1)} %k_ref.1, bf16[3,49,1024]{2,1,0:T(8,128)(2,1)} %v_ref.1, bf16[3,49,1024]{2,1,0:T(8,128)(2,1)} %g_ref.1), custom_call_target="tpu_custom_call" | custom-call | flops 531062784 | bytes 2408448 | tf_op jit(solution)/shard_map/pallas_call | solution.py:350
  38.6 42.8 %shard_map.76 = (bf16[3,49,1024]{2,1,0:T(8,128)(2,1)}, bf16[3,49,1024]{2,1,0:T(8,128)(2,1)}, bf16[3,49,1024]{2,1,0:T(8,128)(2,1)}, bf16[3,49,1024]{2,1,0:T(8,128)(2,1)}) custom-call(bf16[3,49,1024]{2,1,0:T(8,128)(2,1)} %get-tuple-element.8.refs_0_, bf16[3,49,1024]{2,1,0:T(8,128)(2,1)} %get-tuple-element.9.refs_1_, ...), custom_call_target="tpu_custom_call" | custom-call | tf_op jit(solution)/shard_map/pallas_call | solution.py:370

commit v3 on v2

--- a/solution.py
+++ b/solution.py
@@ -349,7 +349,7 @@
         flops = 12 * views * parts * toks * 3 * parts * toks * (width // parts)
         results = pl.pallas_call(
             functools.partial(kernel, groups, parts),
-            out_shape=(shape,) * 4,
+            out_shape=(vmem(queries.shape, BF16),) * 4,
             in_specs=[pl.BlockSpec(memory_space=pl.ANY)] * 4,
             out_specs=[pl.BlockSpec(memory_space=pltpu.VMEM)] * 4,
             scratch_shapes=[
@@ -370,10 +370,10 @@
         return pl.pallas_call(
             deliver,
             out_shape=(shape,) * 4,
-            in_specs=[pl.BlockSpec(memory_space=pl.ANY)] * 4,
+            in_specs=[pl.BlockSpec(memory_space=pltpu.VMEM)] * 4,
             out_specs=[pl.BlockSpec(memory_space=pl.ANY)] * 4,
             scratch_shapes=[dma((4,))],
-            compiler_params=pltpu.CompilerParams(vmem_limit_bytes=58 * 1024 * 1024),
+            compiler_params=pltpu.CompilerParams(vmem_limit_bytes=48 * 1024 * 1024),
         )(*results)
 
     spec = P("view", "tok", None)

time: 81.7 us -> 38.8 us (0.47)
  Pallas kernels: 80.8 us -> 38 us
    pallas_call x1, Pallas kernels: 42.8 us -> 1.11 us  [local(): pl.pallas_call(deliver, out_shape=(shape,) * 4, in_specs=[pl.BlockSpec(me...]
    pallas_call x1, Pallas kernels: 38 us -> 36.9 us  [local(): pl.pallas_call(functools.partial(kernel, groups, parts), out_shape=(vmem(...]
where the time goes in v3:
time: 38.8 us; the launch traced here: 38.6 us
  Pallas kernels  38 us (98%)
  between operations  0.64 us (2%)
    pallas_call x1, Pallas kernels, local(): pl.pallas_call(functools.partial(kernel, groups, parts), out_shape=(vmem(...  36.9 us
    pallas_call x1, Pallas kernels, local(): pl.pallas_call(deliver, out_shape=(shape,) * 4, in_specs=[pl.BlockSpec(me...  1.11 us

profile of v3, /device:TPU:0, one launch (start us, length us, event | category | flops | bytes accessed | tf_op | source)
XLA Modules:
  0.0 38.6 jit_solution(8115105943820552372)
XLA Ops:
  0.6 36.9 %shard_map.75 = (bf16[3,49,1024]{2,1,0:T(8,128)(2,1)S(1)}, bf16[3,49,1024]{2,1,0:T(8,128)(2,1)S(1)}, bf16[3,49,1024]{2,1,0:T(8,128)(2,1)S(1)}, bf16[3,49,1024]{2,1,0:T(8,128)(2,1)S(1)}) custom-call(bf16[3,49,1024]{2,1,0:T(8,128)(2,1)} %q_ref.1, bf16[3,49,1024]{2,1,0:T(8,128)(2,1)} %k_ref.1, bf16[3,49,1024]{2,1,0:T(8,128)(2,1)} %v_ref.1, ...), custom_call_target="tpu_custom_call" | custom-call | flops 531062784 | bytes 2408448 | tf_op jit(solution)/shard_map/pallas_call | solution.py:350
  37.5 1.1 %shard_map.76 = (bf16[3,49,1024]{2,1,0:T(8,128)(2,1)}, bf16[3,49,1024]{2,1,0:T(8,128)(2,1)}, bf16[3,49,1024]{2,1,0:T(8,128)(2,1)}, bf16[3,49,1024]{2,1,0:T(8,128)(2,1)}) custom-call(bf16[3,49,1024]{2,1,0:T(8,128)(2,1)S(1)} %get-tuple-element.8.refs_0_, bf16[3,49,1024]{2,1,0:T(8,128)(2,1)S(1)} %get-tuple-element.9.refs_1_, ...), custom_call_target="tpu_custom_call" | custom-call | tf_op jit(solution)/shard_map/pallas_call | solution.py:370

commit v4 on v3

v4 whole, which is shorter than its diff:
```python
import functools
import math

import jax
import jax.numpy as jnp
from jax import lax
from jax.experimental import pallas as pl
from jax.experimental.pallas import tpu as pltpu
from jax.sharding import PartitionSpec as P

HEADS = 16
PAD = 64
TILE = 16
NEG = -1e30
MESH = pl.DeviceIdType.MESH
F32 = jnp.float32
BF16 = jnp.bfloat16


def kernel(
    groups, parts, q_ref, k_ref, v_ref, g_ref, o_ref, dq_ref, dk_ref, dv_ref,
    qx, gx, kx, vx, in_from, in_to, out_from, out_to, tails, edge, got,
    kvp, kvt, ak, av,
    load_sem, in_send, in_recv, halo_send, halo_recv, part_send, part_recv, out_send, out_recv,
):
    views, toks, width = q_ref.shape
    lanes = kvp.shape[-1]
    half = lanes // 2
    share = width // parts
    chunks = share // lanes
    scale = 1.0 / math.sqrt(half)
    log2e = math.log2(math.e)
    whole8 = toks // 8 * 8
    up8 = (toks + 7) // 8 * 8
    bulk = toks // TILE * TILE
    rest = toks - bulk
    base = 2 * views * bulk
    tail_rows = in_from.shape[-2] - base
    me_v = lax.axis_index("view")
    me_t = lax.axis_index("tok")
    after = lax.rem(me_v + 1, groups)
    before = lax.rem(me_v + groups - 1, groups)
    peers = [lax.rem(me_t + s, parts) for s in range(parts)]

    ins = (q_ref, g_ref, k_ref, v_ref)
    loaded = (qx, gx, kx, vx)
    ROWS, PAIRS = 0, 1
    members = ((0, 1), (2, 3))

    def load(a, s):
        lanes_of = pl.ds(pl.multiple_of(peers[s] * share, lanes), share)
        return pltpu.make_async_copy(
            ins[a].at[:, :, lanes_of], loaded[a].at[s], load_sem.at[s, a]
        )

    for kind in (PAIRS, ROWS):
        for s in reversed(range(parts)):
            for a in members[kind]:
                load(a, s).start()

    barrier = pltpu.get_barrier_semaphore()
    for dev in [(before, me_t), (after, me_t)] + [(me_v, p) for p in peers[1:]]:
        pl.semaphore_signal(barrier, inc=1, device_id=dev, device_id_type=MESH)

    def span(owner, c):
        return pl.ds(pl.multiple_of(owner * share + c * lanes, lanes), lanes)

    def column(c):
        return pl.ds(pl.multiple_of(c * lanes, lanes), lanes)

    def in_copy(kind, c, s):
        return pltpu.make_async_remote_copy(
            src_ref=in_from.at[kind, c, s],
            dst_ref=in_to.at[kind, c, parts - s],
            send_sem=in_send.at[c, s, kind],
            recv_sem=in_recv.at[c, parts - s, kind],
            device_id=(me_v, peers[s]),
            device_id_type=MESH,
        )

    def halo_copy(c, way):
        src, dst, dev = ((1, views + 1, before), (views, 0, after))[way]
        return pltpu.make_async_remote_copy(
            src_ref=kvp.at[c, src],
            dst_ref=kvp.at[c, dst],
            send_sem=halo_send.at[c, way],
            recv_sem=halo_recv.at[c, way],
            device_id=(dev, me_t),
            device_id_type=MESH,
        )

    def part_copy(c, way):
        return pltpu.make_async_remote_copy(
            src_ref=edge.at[c, way],
            dst_ref=got.at[c, way],
            send_sem=part_send.at[c, way],
            recv_sem=part_recv.at[c, way],
            device_id=((before, after)[way], me_t),
            device_id_type=MESH,
        )

    outs = (o_ref, dq_ref, dk_ref, dv_ref)

    def out_copy(kind, c, s):
        return pltpu.make_async_remote_copy(
            src_ref=out_from.at[kind, c, s],
            dst_ref=out_to.at[kind, c, parts - s],
            send_sem=out_send.at[c, s, kind],
            recv_sem=out_recv.at[c, parts - s, kind],
            device_id=(me_v, peers[s]),
            device_id_type=MESH,
        )

    tail_row = lax.broadcasted_iota(jnp.int32, (tail_rows, lanes), 0)

    def send_in(kind, c):
        for s in range(1, parts):
            tail = jnp.zeros((tail_rows, lanes), F32)
            for i, a in enumerate(members[kind]):
                for v in range(views):
                    at = i * views + v
                    block = loaded[a][s, v, :, column(c)]
                    in_from[kind, c, s, at * bulk : (at + 1) * bulk] = block[:bulk]
                    for r in range(rest):
                        row = block[bulk + r : bulk + r + 1].astype(F32)
                        tail = jnp.where(tail_row == at * rest + r, row, tail)
            in_from[kind, c, s, base:] = tail.astype(BF16)
            in_copy(kind, c, s).start()

    for kind in (PAIRS, ROWS):
        for s in reversed(range(1, parts)):
            for a in members[kind]:
                load(a, s).wait()
        if kind == PAIRS:
            pl.semaphore_wait(barrier, parts + 1)
        send_in(kind, 0)
    if chunks > 1:
        send_in(PAIRS, 1)

    @pl.loop(1, chunks)
    def _(c):
        @pl.when(c + 1 < chunks)
        def _():
            send_in(PAIRS, c + 1)

        send_in(ROWS, c)

    for a in range(4):
        load(a, 0).wait()

    pad_row = lax.broadcasted_iota(jnp.int32, (PAD - bulk, lanes), 0)

    def blocks_of(kind, i, c, s, v):
        if s == 0:
            block = loaded[members[kind][i]][0, v, :, column(c)]
            return jnp.concatenate([block, jnp.zeros((PAD - toks, lanes), BF16)], axis=0)
        at = i * views + v
        tail = in_to[kind, c, s, base:].astype(F32)
        end = jnp.zeros((PAD - bulk, lanes), F32)
        for r in range(rest):
            end = jnp.where(pad_row == r, tail[at * rest + r : at * rest + r + 1], end)
        main = in_to[kind, c, s, at * bulk : (at + 1) * bulk]
        return jnp.concatenate([main, end.astype(BF16)], axis=0)

    def relay(c):
        for s in range(1, parts):
            in_copy(PAIRS, c, parts - s).wait_recv()
        for v in range(views):
            for a in range(2):
                rows = [blocks_of(PAIRS, a, c, s, v) for s in range(parts)]
                kvp[c, v + 1, a] = jnp.concatenate(rows, axis=0)
        for way in range(2):
            halo_copy(c, way).start()
        for w in range(1, views + 1):
            turn(c, w)

    def turn(c, w):
        for a in range(2):
            kvt[c, w, a] = kvp[c, w, a].T

    def queries_ready(c):
        for s in range(1, parts):
            in_copy(ROWS, c, parts - s).wait_recv()

    def stage_halo(c):
        for way in range(2):
            halo_copy(c, way).wait_recv()
        turn(c, 0)
        turn(c, views + 1)

    def put(kind, i, c, s, v, block):
        at = i * views + v
        out_from[kind, c, s, at * bulk : (at + 1) * bulk] = block[:bulk].astype(BF16)
        for r in range(rest):
            row = at * rest + r
            tails[kind, s, row : row + 1] = block[bulk + r : bulk + r + 1]

    def send_out(kind, c):
        for s in range(1, parts):
            out_from[kind, c, s, base:] = tails[kind, s].astype(BF16)
            out_copy(kind, c, s).start()

    def take(kind, c, s):
        tail = out_to[kind, c, s, base:].astype(F32)
        for i, ref in enumerate(((o_ref, dq_ref), (dk_ref, dv_ref))[kind]):
            for v in range(views):
                at = i * views + v
                ref[v, :bulk, span(peers[s], c)] = out_to[kind, c, s, at * bulk : (at + 1) * bulk]
                if rest:
                    rows = tail[at * rest : (at + 1) * rest]
                    ref[v, bulk:toks, span(peers[s], c)] = rows.astype(BF16)

    lane = lax.broadcasted_iota(jnp.int32, (2 * PAD, lanes), 1)
    row_ok = lax.broadcasted_iota(jnp.int32, (up8 - whole8, 2 * lanes), 0) < toks - whole8
    blocks = 3 * parts

    def twin(x):
        zero = jnp.zeros_like(x)
        return jnp.concatenate([jnp.where(lane < half, x, zero), jnp.where(lane < half, zero, x)], 0)

    def full(x):
        filler = jnp.zeros((blocks, PAD - up8, 2 * lanes), F32)
        return jnp.concatenate([x, filler], axis=1).reshape(blocks * PAD, 2 * lanes).astype(BF16)

    def diagonal(x):
        return jnp.concatenate([x[:half, :lanes], x[half:, lanes:]], axis=0).T

    def dot(x, y):
        return jnp.dot(x, y, preferred_element_type=F32)

    def dot_t(x, y):
        return lax.dot_general(x, y, (((1,), (1,)), ((), ())), preferred_element_type=F32)

    def compute(c, v):
        now = lax.rem(c, 2)
        key_rows, value_rows = (
            jnp.concatenate([kvp[c, v + j, a] for j in range(3)], axis=0) for a in range(2)
        )
        key_cols, value_cols = (
            jnp.concatenate([kvt[c, v + j, a] for j in range(3)], axis=1) for a in range(2)
        )
        for s in range(0, parts, 2):
            query = jnp.concatenate([blocks_of(ROWS, 0, c, s + i, v) for i in range(2)], axis=0)
            grad = jnp.concatenate([blocks_of(ROWS, 1, c, s + i, v) for i in range(2)], axis=0)
            query = twin(query * jnp.asarray(scale, BF16))
            grad = twin(grad)
            scores = dot_t(key_rows, query).reshape(blocks, PAD, 2 * lanes)
            tail = jnp.where(row_ok[None], scores[:, whole8:up8], NEG)
            scores = jnp.concatenate([scores[:, :whole8], tail], axis=1)
            top = jnp.max(scores, axis=(0, 1), keepdims=True)
            probs = jnp.exp2((scores - top) * log2e)
            probs = probs * (1.0 / jnp.sum(probs, axis=(0, 1), keepdims=True))
            grad_probs = dot_t(value_rows, grad).reshape(blocks, PAD, 2 * lanes)[:, :up8]
            weighted = probs * grad_probs
            delta = jnp.sum(weighted, axis=(0, 1), keepdims=True)
            probs_bf = full(probs)
            grad_bf = full(weighted - probs * delta)
            key_term = dot(grad_bf, query).reshape(3, parts * PAD, lanes)
            value_term = dot(probs_bf, grad).reshape(3, parts * PAD, lanes)
            ak[now, v : v + 3] += key_term
            av[now, v : v + 3] += value_term
            attended = diagonal(dot(value_cols, probs_bf))
            query_grad = diagonal(dot(key_cols, grad_bf)) * scale
            for i in range(2):
                rows = slice(i * PAD, i * PAD + toks)
                if s + i == 0:
                    o_ref[v, :, span(me_t, c)] = attended[rows].astype(BF16)
                    dq_ref[v, :, span(me_t, c)] = query_grad[rows].astype(BF16)
                else:
                    put(ROWS, 0, c, s + i, v, attended[rows])
                    put(ROWS, 1, c, s + i, v, query_grad[rows])

    def clear(c):
        now = lax.rem(c, 2)
        ak[now] = jnp.zeros(ak.shape[1:], F32)
        av[now] = jnp.zeros(av.shape[1:], F32)

    def middle(c):
        for v in range(1, views - 1):
            compute(c, v)

    def edges(c):
        compute(c, 0)
        if views > 1:
            compute(c, views - 1)
        now = lax.rem(c, 2)
        for way, w in enumerate((0, views + 1)):
            for a, sums in enumerate((ak, av)):
                for s in range(parts):
                    edge[c, way, a, s] = sums[now, w, s * PAD : s * PAD + toks].astype(BF16)
            part_copy(c, way).start()

    def finish(c):
        now = lax.rem(c, 2)
        for way in range(2):
            part_copy(c, way).wait_recv()
        for s in reversed(range(parts)):
            for a, (sums, ref) in enumerate(((ak, dk_ref), (av, dv_ref))):
                for v in range(views):
                    total = sums[now, v + 1, s * PAD : s * PAD + toks]
                    if v == 0:
                        total = total + got[c, 1, a, s].astype(F32)
                    if v == views - 1:
                        total = total + got[c, 0, a, s].astype(F32)
                    if s == 0:
                        ref[v, :, span(me_t, c)] = total.astype(BF16)
                    else:
                        put(PAIRS, a, c, s, v, total)
            if s == 1:
                send_out(PAIRS, c)

    tails[...] = jnp.zeros_like(tails)
    relay(0)
    clear(0)
    queries_ready(0)
    middle(0)
    if chunks > 1:
        relay(1)
    stage_halo(0)
    edges(0)
    send_out(ROWS, 0)

    @pl.loop(1, chunks)
    def _(c):
        clear(c)

        @pl.when(c + 1 < chunks)
        def _():
            relay(c + 1)

        queries_ready(c)
        stage_halo(c)
        edges(c)
        finish(c - 1)
        middle(c)
        send_out(ROWS, c)

    finish(chunks - 1)

    @pl.loop(0, chunks)
    def _(c):
        for kind in range(2):
            for s in range(1, parts):
                in_copy(kind, c, s).wait_send()
                out_copy(kind, c, s).wait_send()
                out_copy(kind, c, parts - s).wait_recv()
                take(kind, c, s)
        for way in range(2):
            part_copy(c, way).wait_send()
            halo_copy(c, way).wait_send()


def deliver(*refs):
    count = len(refs) // 2
    copies = [
        pltpu.make_async_copy(refs[i], refs[count + i], refs[-1].at[i]) for i in range(count)
    ]
    for copy in copies:
        copy.start()
    for copy in copies:
        copy.wait()


def solution(mesh):
    groups, parts = mesh.shape["view"], mesh.shape["tok"]

    def local(queries, keys, values, grad_out):
        views, toks, width = queries.shape
        lanes = 2 * (width // HEADS)
        chunks = width // parts // lanes
        vmem = pltpu.VMEM
        dma = pltpu.SemaphoreType.DMA
        bulk = toks // TILE * TILE
        tail = (2 * views * (toks - bulk) + TILE - 1) // TILE * TILE
        source = vmem((parts, views, toks, width // parts), BF16)
        packed = vmem((2, chunks, parts, 2 * views * bulk + tail, lanes), BF16)
        edge = vmem((chunks, 2, 2, parts, toks, lanes), BF16)
        rows = vmem((chunks, views + 2, 2, parts * PAD, lanes), BF16)
        cols = vmem((chunks, views + 2, 2, lanes, parts * PAD), BF16)
        sums = vmem((2, views + 2, parts * PAD, lanes), F32)
        shape = jax.ShapeDtypeStruct(queries.shape, BF16)
        flops = 12 * views * parts * toks * 3 * parts * toks * (width // parts)
        results = pl.pallas_call(
            functools.partial(kernel, groups, parts),
            out_shape=(vmem(queries.shape, BF16),) * 4,
            in_specs=[pl.BlockSpec(memory_space=pl.ANY)] * 4,
            out_specs=[pl.BlockSpec(memory_space=pltpu.VMEM)] * 4,
            scratch_shapes=[
                source, source, source, source, packed, packed, packed, packed,
                vmem((2, parts, tail, lanes), F32), edge, edge, rows, cols, sums, sums,
                dma((parts, 4)), dma((chunks, parts, 2)), dma((chunks, parts, 2)),
                dma((chunks, 2)), dma((chunks, 2)), dma((chunks, 2)), dma((chunks, 2)),
                dma((chunks, parts, 2)), dma((chunks, parts, 2)),
            ],
            cost_estimate=pl.CostEstimate(
                flops=flops, bytes_accessed=16 * views * toks * width, transcendentals=0
            ),
            compiler_params=pltpu.CompilerParams(
                collective_id=0, has_side_effects=True, vmem_limit_bytes=58 * 1024 * 1024
            ),
        )(queries, keys, values, grad_out)
        return pl.pallas_call(
            deliver,
            out_shape=(shape,) * 4,
            in_specs=[pl.BlockSpec(memory_space=pltpu.VMEM)] * 4,
            out_specs=[pl.BlockSpec(memory_space=pl.ANY)] * 4,
            scratch_shapes=[dma((4,))],
            compiler_params=pltpu.CompilerParams(vmem_limit_bytes=48 * 1024 * 1024),
        )(*results)

    spec = P("view", "tok", None)
    return jax.shard_map(
        local, mesh=mesh, in_specs=(spec,) * 4, out_specs=(spec,) * 4, check_vma=False
    )
```

time: 38.8 us -> 36.3 us (0.936)
  Pallas kernels: 38 us -> 35.5 us
    pallas_call x1, Pallas kernels: 36.9 us -> 34.4 us  [local(): pl.pallas_call(functools.partial(kernel, groups, parts), out_shape=(vmem(...]
where the time goes in v4:
time: 36.3 us; the launch traced here: 36.1 us
  Pallas kernels  35.5 us (98%)
  between operations  0.64 us (2%)
    pallas_call x1, Pallas kernels, local(): pl.pallas_call(functools.partial(kernel, groups, parts), out_shape=(vmem(...  34.4 us
    pallas_call x1, Pallas kernels, local(): pl.pallas_call(deliver, out_shape=(shape,) * 4, in_specs=[pl.BlockSpec(me...  1.11 us

profile of v4, /device:TPU:0, one launch (start us, length us, event | category | flops | bytes accessed | tf_op | source)
XLA Modules:
  0.0 36.1 jit_solution(4999292389971672833)
XLA Ops:
  0.6 34.4 %shard_map.75 = (bf16[3,49,1024]{2,1,0:T(8,128)(2,1)S(1)}, bf16[3,49,1024]{2,1,0:T(8,128)(2,1)S(1)}, bf16[3,49,1024]{2,1,0:T(8,128)(2,1)S(1)}, bf16[3,49,1024]{2,1,0:T(8,128)(2,1)S(1)}) custom-call(bf16[3,49,1024]{2,1,0:T(8,128)(2,1)} %q_ref.1, bf16[3,49,1024]{2,1,0:T(8,128)(2,1)} %k_ref.1, bf16[3,49,1024]{2,1,0:T(8,128)(2,1)} %v_ref.1, ...), custom_call_target="tpu_custom_call" | custom-call | flops 531062784 | bytes 2408448 | tf_op jit(solution)/shard_map/pallas_call | solution.py:383
  35.0 1.1 %shard_map.76 = (bf16[3,49,1024]{2,1,0:T(8,128)(2,1)}, bf16[3,49,1024]{2,1,0:T(8,128)(2,1)}, bf16[3,49,1024]{2,1,0:T(8,128)(2,1)}, bf16[3,49,1024]{2,1,0:T(8,128)(2,1)}) custom-call(bf16[3,49,1024]{2,1,0:T(8,128)(2,1)S(1)} %get-tuple-element.8.refs_0_, bf16[3,49,1024]{2,1,0:T(8,128)(2,1)S(1)} %get-tuple-element.9.refs_1_, ...), custom_call_target="tpu_custom_call" | custom-call | tf_op jit(solution)/shard_map/pallas_call | solution.py:402

commit v5 on v4

--- a/solution.py
+++ b/solution.py
@@ -231,58 +231,68 @@
     def dot_t(x, y):
         return lax.dot_general(x, y, (((1,), (1,)), ((), ())), preferred_element_type=F32)
 
-    def compute(c, v):
-        now = lax.rem(c, 2)
+    def front(c, v, s):
         key_rows, value_rows = (
             jnp.concatenate([kvp[c, v + j, a] for j in range(3)], axis=0) for a in range(2)
         )
+        query = jnp.concatenate([blocks_of(ROWS, 0, c, s + i, v) for i in range(2)], axis=0)
+        grad = jnp.concatenate([blocks_of(ROWS, 1, c, s + i, v) for i in range(2)], axis=0)
+        query = twin(query * jnp.asarray(scale, BF16))
+        grad = twin(grad)
+        scores = dot_t(key_rows, query).reshape(blocks, PAD, 2 * lanes)
+        tail = jnp.where(row_ok[None], scores[:, whole8:up8], NEG)
+        scores = jnp.concatenate([scores[:, :whole8], tail], axis=1)
+        top = jnp.max(scores, axis=(0, 1), keepdims=True)
+        probs = jnp.exp2((scores - top) * log2e)
+        probs = probs * (1.0 / jnp.sum(probs, axis=(0, 1), keepdims=True))
+        grad_probs = dot_t(value_rows, grad).reshape(blocks, PAD, 2 * lanes)[:, :up8]
+        weighted = probs * grad_probs
+        delta = jnp.sum(weighted, axis=(0, 1), keepdims=True)
+        return query, grad, full(probs), full(weighted - probs * delta)
+
+    def back(c, v, s, query, grad, probs_bf, grad_bf):
+        now = lax.rem(c, 2)
         key_cols, value_cols = (
             jnp.concatenate([kvt[c, v + j, a] for j in range(3)], axis=1) for a in range(2)
         )
-        for s in range(0, parts, 2):
-            query = jnp.concatenate([blocks_of(ROWS, 0, c, s + i, v) for i in range(2)], axis=0)
-            grad = jnp.concatenate([blocks_of(ROWS, 1, c, s + i, v) for i in range(2)], axis=0)
-            query = twin(query * jnp.asarray(scale, BF16))
-            grad = twin(grad)
-            scores = dot_t(key_rows, query).reshape(blocks, PAD, 2 * lanes)
-            tail = jnp.where(row_ok[None], scores[:, whole8:up8], NEG)
-            scores = jnp.concatenate([scores[:, :whole8], tail], axis=1)
-            top = jnp.max(scores, axis=(0, 1), keepdims=True)
-            probs = jnp.exp2((scores - top) * log2e)
-            probs = probs * (1.0 / jnp.sum(probs, axis=(0, 1), keepdims=True))
-            grad_probs = dot_t(value_rows, grad).reshape(blocks, PAD, 2 * lanes)[:, :up8]
-            weighted = probs * grad_probs
-            delta = jnp.sum(weighted, axis=(0, 1), keepdims=True)
-            probs_bf = full(probs)
-            grad_bf = full(weighted - probs * delta)
-            key_term = dot(grad_bf, query).reshape(3, parts * PAD, lanes)
-            value_term = dot(probs_bf, grad).reshape(3, parts * PAD, lanes)
-            ak[now, v : v + 3] += key_term
-            av[now, v : v + 3] += value_term
-            attended = diagonal(dot(value_cols, probs_bf))
-            query_grad = diagonal(dot(key_cols, grad_bf)) * scale
-            for i in range(2):
-                rows = slice(i * PAD, i * PAD + toks)
-                if s + i == 0:
-                    o_ref[v, :, span(me_t, c)] = attended[rows].astype(BF16)
-                    dq_ref[v, :, span(me_t, c)] = query_grad[rows].astype(BF16)
-                else:
-                    put(ROWS, 0, c, s + i, v, attended[rows])
-                    put(ROWS, 1, c, s + i, v, query_grad[rows])
+        ak[now, v : v + 3] += dot(grad_bf, query).reshape(3, parts * PAD, lanes)
+        av[now, v : v + 3] += dot(probs_bf, grad).reshape(3, parts * PAD, lanes)
+        attended = diagonal(dot(value_cols, probs_bf))
+        query_grad = diagonal(dot(key_cols, grad_bf)) * scale
+        for i in range(2):
+            rows = slice(i * PAD, i * PAD + toks)
+            if s + i == 0:
+                o_ref[v, :, span(me_t, c)] = attended[rows].astype(BF16)
+                dq_ref[v, :, span(me_t, c)] = query_grad[rows].astype(BF16)
+            else:
+                put(ROWS, 0, c, s + i, v, attended[rows])
+                put(ROWS, 1, c, s + i, v, query_grad[rows])
+
+    def compute(c, edge_views, inner_views):
+        tasks = [(v, s) for v in edge_views + inner_views for s in range(0, parts, 2)]
+        last_edge = len(edge_views) * (parts // 2)
+        held = None
+        for at, (v, s) in enumerate(tasks):
+            made = front(c, v, s)
+            if held is not None:
+                back(c, *tasks[at - 1], *held)
+                if at == last_edge:
+                    send_parts(c)
+            held = made
+        if held is not None:
+            back(c, *tasks[-1], *held)
+        if len(tasks) == last_edge and last_edge:
+            send_parts(c)
 
     def clear(c):
         now = lax.rem(c, 2)
         ak[now] = jnp.zeros(ak.shape[1:], F32)
         av[now] = jnp.zeros(av.shape[1:], F32)
 
-    def middle(c):
-        for v in range(1, views - 1):
-            compute(c, v)
-
-    def edges(c):
-        compute(c, 0)
-        if views > 1:
-            compute(c, views - 1)
+    edge_views = [0, views - 1][: min(views, 2)]
+    inner_views = list(range(1, views - 1))
+
+    def send_parts(c):
         now = lax.rem(c, 2)
         for way, w in enumerate((0, views + 1)):
             for a, sums in enumerate((ak, av)):
@@ -313,11 +323,11 @@
     relay(0)
     clear(0)
     queries_ready(0)
-    middle(0)
+    compute(0, [], inner_views)
     if chunks > 1:
         relay(1)
     stage_halo(0)
-    edges(0)
+    compute(0, edge_views, [])
     send_out(ROWS, 0)
 
     @pl.loop(1, chunks)
@@ -330,10 +340,9 @@
 
         queries_ready(c)
         stage_halo(c)
-        edges(c)
+        compute(c, edge_views, inner_views)
+        send_out(ROWS, c)
         finish(c - 1)
-        middle(c)
-        send_out(ROWS, c)
 
     finish(chunks - 1)
 
@@ -353,7 +362,9 @@
 def deliver(*refs):
     count = len(refs) // 2
     copies = [
-        pltpu.make_async_copy(refs[i], refs[count + i], refs[-1].at[i]) for i in range(count)
+        pltpu.make_async_copy(refs[i].at[v], refs[count + i].at[v], refs[-1].at[i, v])
+        for i in range(count)
+        for v in range(refs[0].shape[0])
     ]
     for copy in copies:
         copy.start()
@@ -371,7 +382,7 @@
         vmem = pltpu.VMEM
         dma = pltpu.SemaphoreType.DMA
         bulk = toks // TILE * TILE
-        tail = (2 * views * (toks - bulk) + TILE - 1) // TILE * TILE
+        tail = (2 * views * (toks - bulk) + 7) // 8 * 8
         source = vmem((parts, views, toks, width // parts), BF16)
         packed = vmem((2, chunks, parts, 2 * views * bulk + tail, lanes), BF16)
         edge = vmem((chunks, 2, 2, parts, toks, lanes), BF16)
@@ -404,7 +415,7 @@
             out_shape=(shape,) * 4,
             in_specs=[pl.BlockSpec(memory_space=pltpu.VMEM)] * 4,
             out_specs=[pl.BlockSpec(memory_space=pl.ANY)] * 4,
-            scratch_shapes=[dma((4,))],
+            scratch_shapes=[dma((4, views))],
             compiler_params=pltpu.CompilerParams(vmem_limit_bytes=48 * 1024 * 1024),
         )(*results)
 

time: 36.3 us -> 34.9 us (0.961)
  Pallas kernels: 35.5 us -> 34.1 us
    pallas_call x1, Pallas kernels: 34.4 us -> 32.9 us  [local(): pl.pallas_call(functools.partial(kernel, groups, parts), out_shape=(vmem(...]
where the time goes in v5:
time: 34.9 us; the launch traced here: 34.7 us
  Pallas kernels  34.1 us (98%)
  between operations  0.64 us (2%)
    pallas_call x1, Pallas kernels, local(): pl.pallas_call(functools.partial(kernel, groups, parts), out_shape=(vmem(...  32.9 us
    pallas_call x1, Pallas kernels, local(): pl.pallas_call(deliver, out_shape=(shape,) * 4, in_specs=[pl.BlockSpec(me...  1.17 us

profile of v5, /device:TPU:0, one launch (start us, length us, event | category | flops | bytes accessed | tf_op | source)
XLA Modules:
  0.0 34.7 jit_solution(13175048439085625864)
XLA Ops:
  0.6 32.9 %shard_map.75 = (bf16[3,49,1024]{2,1,0:T(8,128)(2,1)S(1)}, bf16[3,49,1024]{2,1,0:T(8,128)(2,1)S(1)}, bf16[3,49,1024]{2,1,0:T(8,128)(2,1)S(1)}, bf16[3,49,1024]{2,1,0:T(8,128)(2,1)S(1)}) custom-call(bf16[3,49,1024]{2,1,0:T(8,128)(2,1)} %q_ref.1, bf16[3,49,1024]{2,1,0:T(8,128)(2,1)} %k_ref.1, bf16[3,49,1024]{2,1,0:T(8,128)(2,1)} %v_ref.1, ...), custom_call_target="tpu_custom_call" | custom-call | flops 531062784 | bytes 2408448 | tf_op jit(solution)/shard_map/pallas_call | solution.py:394
  33.6 1.2 %shard_map.76 = (bf16[3,49,1024]{2,1,0:T(8,128)(2,1)}, bf16[3,49,1024]{2,1,0:T(8,128)(2,1)}, bf16[3,49,1024]{2,1,0:T(8,128)(2,1)}, bf16[3,49,1024]{2,1,0:T(8,128)(2,1)}) custom-call(bf16[3,49,1024]{2,1,0:T(8,128)(2,1)S(1)} %get-tuple-element.8.refs_0_, bf16[3,49,1024]{2,1,0:T(8,128)(2,1)S(1)} %get-tuple-element.9.refs_1_, ...), custom_call_target="tpu_custom_call" | custom-call | tf_op jit(solution)/shard_map/pallas_call | solution.py:413

commit v6 on v5

--- a/solution.py
+++ b/solution.py
@@ -137,14 +137,6 @@
     if chunks > 1:
         send_in(PAIRS, 1)
 
-    @pl.loop(1, chunks)
-    def _(c):
-        @pl.when(c + 1 < chunks)
-        def _():
-            send_in(PAIRS, c + 1)
-
-        send_in(ROWS, c)
-
     for a in range(4):
         load(a, 0).wait()
 
@@ -321,11 +313,17 @@
 
     tails[...] = jnp.zeros_like(tails)
     relay(0)
+    if chunks > 2:
+        send_in(PAIRS, 2)
     clear(0)
     queries_ready(0)
+    if chunks > 1:
+        send_in(ROWS, 1)
     compute(0, [], inner_views)
     if chunks > 1:
         relay(1)
+    if chunks > 3:
+        send_in(PAIRS, 3)
     stage_halo(0)
     compute(0, edge_views, [])
     send_out(ROWS, 0)
@@ -337,8 +335,14 @@
         @pl.when(c + 1 < chunks)
         def _():
             relay(c + 1)
+            send_in(ROWS, c + 1)
 
         queries_ready(c)
+
+        @pl.when(c + 3 < chunks)
+        def _():
+            send_in(PAIRS, c + 3)
+
         stage_halo(c)
         compute(c, edge_views, inner_views)
         send_out(ROWS, c)
@@ -362,9 +366,7 @@
 def deliver(*refs):
     count = len(refs) // 2
     copies = [
-        pltpu.make_async_copy(refs[i].at[v], refs[count + i].at[v], refs[-1].at[i, v])
-        for i in range(count)
-        for v in range(refs[0].shape[0])
+        pltpu.make_async_copy(refs[i], refs[count + i], refs[-1].at[i]) for i in range(count)
     ]
     for copy in copies:
         copy.start()
@@ -415,7 +417,7 @@
             out_shape=(shape,) * 4,
             in_specs=[pl.BlockSpec(memory_space=pltpu.VMEM)] * 4,
             out_specs=[pl.BlockSpec(memory_space=pl.ANY)] * 4,
-            scratch_shapes=[dma((4, views))],
+            scratch_shapes=[dma((4,))],
             compiler_params=pltpu.CompilerParams(vmem_limit_bytes=48 * 1024 * 1024),
         )(*results)
 

time: 34.9 us -> 36.8 us (1.054)
  Pallas kernels: 34.1 us -> 36 us
    pallas_call x1, Pallas kernels: 32.9 us -> 34.9 us  [local(): pl.pallas_call(functools.partial(kernel, groups, parts), out_shape=(vmem(...]
where the time goes in v6:
time: 36.8 us; the launch traced here: 36.7 us
  Pallas kernels  36 us (98%)
  between operations  0.64 us (2%)
    pallas_call x1, Pallas kernels, local(): pl.pallas_call(functools.partial(kernel, groups, parts), out_shape=(vmem(...  34.9 us
    pallas_call x1, Pallas kernels, local(): pl.pallas_call(deliver, out_shape=(shape,) * 4, in_specs=[pl.BlockSpec(me...  1.11 us

profile of v6, /device:TPU:0, one launch (start us, length us, event | category | flops | bytes accessed | tf_op | source)
XLA Modules:
  0.0 36.7 jit_solution(11610896718054123997)
XLA Ops:
  0.6 34.9 %shard_map.75 = (bf16[3,49,1024]{2,1,0:T(8,128)(2,1)S(1)}, bf16[3,49,1024]{2,1,0:T(8,128)(2,1)S(1)}, bf16[3,49,1024]{2,1,0:T(8,128)(2,1)S(1)}, bf16[3,49,1024]{2,1,0:T(8,128)(2,1)S(1)}) custom-call(bf16[3,49,1024]{2,1,0:T(8,128)(2,1)} %q_ref.1, bf16[3,49,1024]{2,1,0:T(8,128)(2,1)} %k_ref.1, bf16[3,49,1024]{2,1,0:T(8,128)(2,1)} %v_ref.1, ...), custom_call_target="tpu_custom_call" | custom-call | flops 531062784 | bytes 2408448 | tf_op jit(solution)/shard_map/pallas_call | solution.py:396
  35.6 1.1 %shard_map.76 = (bf16[3,49,1024]{2,1,0:T(8,128)(2,1)}, bf16[3,49,1024]{2,1,0:T(8,128)(2,1)}, bf16[3,49,1024]{2,1,0:T(8,128)(2,1)}, bf16[3,49,1024]{2,1,0:T(8,128)(2,1)}) custom-call(bf16[3,49,1024]{2,1,0:T(8,128)(2,1)S(1)} %get-tuple-element.8.refs_0_, bf16[3,49,1024]{2,1,0:T(8,128)(2,1)S(1)} %get-tuple-element.9.refs_1_, ...), custom_call_target="tpu_custom_call" | custom-call | tf_op jit(solution)/shard_map/pallas_call | solution.py:415

commit v7 on v5

--- a/solution.py
+++ b/solution.py
@@ -195,10 +195,28 @@
             row = at * rest + r
             tails[kind, s, row : row + 1] = block[bulk + r : bulk + r + 1]
 
-    def send_out(kind, c):
+    def start_out(kind, c):
+        for s in range(1, parts):
+            out_copy(kind, c, s).start()
+
+    def send_out(kind, c, step):
         for s in range(1, parts):
             out_from[kind, c, s, base:] = tails[kind, s].astype(BF16)
-            out_copy(kind, c, s).start()
+
+        @pl.when(step >= chunks - 2)
+        def _():
+            start_out(kind, c)
+
+    def flush(step):
+        @pl.when(step == chunks - 2)
+        def _():
+            @pl.loop(0, chunks - 2)
+            def _(c):
+                start_out(ROWS, c)
+
+                @pl.when(c < chunks - 3)
+                def _():
+                    start_out(PAIRS, c)
 
     def take(kind, c, s):
         tail = out_to[kind, c, s, base:].astype(F32)
@@ -268,7 +286,7 @@
                 put(ROWS, 0, c, s + i, v, attended[rows])
                 put(ROWS, 1, c, s + i, v, query_grad[rows])
 
-    def compute(c, edge_views, inner_views):
+    def compute(c, edge_views, inner_views, between=lambda: None):
         tasks = [(v, s) for v in edge_views + inner_views for s in range(0, parts, 2)]
         last_edge = len(edge_views) * (parts // 2)
         held = None
@@ -278,11 +296,13 @@
                 back(c, *tasks[at - 1], *held)
                 if at == last_edge:
                     send_parts(c)
+                    between()
             held = made
         if held is not None:
             back(c, *tasks[-1], *held)
         if len(tasks) == last_edge and last_edge:
             send_parts(c)
+            between()
 
     def clear(c):
         now = lax.rem(c, 2)
@@ -300,7 +320,7 @@
                     edge[c, way, a, s] = sums[now, w, s * PAD : s * PAD + toks].astype(BF16)
             part_copy(c, way).start()
 
-    def finish(c):
+    def finish(c, step):
         now = lax.rem(c, 2)
         for way in range(2):
             part_copy(c, way).wait_recv()
@@ -317,7 +337,7 @@
                     else:
                         put(PAIRS, a, c, s, v, total)
             if s == 1:
-                send_out(PAIRS, c)
+                send_out(PAIRS, c, step)
 
     tails[...] = jnp.zeros_like(tails)
     relay(0)
@@ -328,7 +348,7 @@
         relay(1)
     stage_halo(0)
     compute(0, edge_views, [])
-    send_out(ROWS, 0)
+    send_out(ROWS, 0, 0)
 
     @pl.loop(1, chunks)
     def _(c):
@@ -339,12 +359,12 @@
             relay(c + 1)
 
         queries_ready(c)
+        flush(c)
         stage_halo(c)
-        compute(c, edge_views, inner_views)
-        send_out(ROWS, c)
-        finish(c - 1)
-
-    finish(chunks - 1)
+        compute(c, edge_views, inner_views, lambda: finish(c - 1, c))
+        send_out(ROWS, c, c)
+
+    finish(chunks - 1, chunks)
 
     @pl.loop(0, chunks)
     def _(c):
@@ -362,9 +382,7 @@
 def deliver(*refs):
     count = len(refs) // 2
     copies = [
-        pltpu.make_async_copy(refs[i].at[v], refs[count + i].at[v], refs[-1].at[i, v])
-        for i in range(count)
-        for v in range(refs[0].shape[0])
+        pltpu.make_async_copy(refs[i], refs[count + i], refs[-1].at[i]) for i in range(count)
     ]
     for copy in copies:
         copy.start()
@@ -415,7 +433,7 @@
             out_shape=(shape,) * 4,
             in_specs=[pl.BlockSpec(memory_space=pltpu.VMEM)] * 4,
             out_specs=[pl.BlockSpec(memory_space=pl.ANY)] * 4,
-            scratch_shapes=[dma((4, views))],
+            scratch_shapes=[dma((4,))],
             compiler_params=pltpu.CompilerParams(vmem_limit_bytes=48 * 1024 * 1024),
         )(*results)
 

time: 34.9 us -> 35.3 us (1.011)
  Pallas kernels: 34.1 us -> 34.5 us
    pallas_call x1, Pallas kernels: 32.9 us -> 33.4 us  [local(): pl.pallas_call(functools.partial(kernel, groups, parts), out_shape=(vmem(...]
where the time goes in v7:
time: 35.3 us; the launch traced here: 35.1 us
  Pallas kernels  34.5 us (98%)
  between operations  0.64 us (2%)
    pallas_call x1, Pallas kernels, local(): pl.pallas_call(functools.partial(kernel, groups, parts), out_shape=(vmem(...  33.4 us
    pallas_call x1, Pallas kernels, local(): pl.pallas_call(deliver, out_shape=(shape,) * 4, in_specs=[pl.BlockSpec(me...  1.11 us

profile of v7, /device:TPU:0, one launch (start us, length us, event | category | flops | bytes accessed | tf_op | source)
XLA Modules:
  0.0 35.1 jit_solution(16796901836485001028)
XLA Ops:
  0.6 33.4 %shard_map.75 = (bf16[3,49,1024]{2,1,0:T(8,128)(2,1)S(1)}, bf16[3,49,1024]{2,1,0:T(8,128)(2,1)S(1)}, bf16[3,49,1024]{2,1,0:T(8,128)(2,1)S(1)}, bf16[3,49,1024]{2,1,0:T(8,128)(2,1)S(1)}) custom-call(bf16[3,49,1024]{2,1,0:T(8,128)(2,1)} %q_ref.1, bf16[3,49,1024]{2,1,0:T(8,128)(2,1)} %k_ref.1, bf16[3,49,1024]{2,1,0:T(8,128)(2,1)} %v_ref.1, ...), custom_call_target="tpu_custom_call" | custom-call | flops 531062784 | bytes 2408448 | tf_op jit(solution)/shard_map/pallas_call | solution.py:412
  34.0 1.1 %shard_map.76 = (bf16[3,49,1024]{2,1,0:T(8,128)(2,1)}, bf16[3,49,1024]{2,1,0:T(8,128)(2,1)}, bf16[3,49,1024]{2,1,0:T(8,128)(2,1)}, bf16[3,49,1024]{2,1,0:T(8,128)(2,1)}) custom-call(bf16[3,49,1024]{2,1,0:T(8,128)(2,1)S(1)} %get-tuple-element.8.refs_0_, bf16[3,49,1024]{2,1,0:T(8,128)(2,1)S(1)} %get-tuple-element.9.refs_1_, ...), custom_call_target="tpu_custom_call" | custom-call | tf_op jit(solution)/shard_map/pallas_call | solution.py:431

commit v8 on v5

--- a/solution.py
+++ b/solution.py
@@ -268,7 +268,7 @@
                 put(ROWS, 0, c, s + i, v, attended[rows])
                 put(ROWS, 1, c, s + i, v, query_grad[rows])
 
-    def compute(c, edge_views, inner_views):
+    def compute(c, edge_views, inner_views, between=lambda: None):
         tasks = [(v, s) for v in edge_views + inner_views for s in range(0, parts, 2)]
         last_edge = len(edge_views) * (parts // 2)
         held = None
@@ -278,11 +278,13 @@
                 back(c, *tasks[at - 1], *held)
                 if at == last_edge:
                     send_parts(c)
+                    between()
             held = made
         if held is not None:
             back(c, *tasks[-1], *held)
         if len(tasks) == last_edge and last_edge:
             send_parts(c)
+            between()
 
     def clear(c):
         now = lax.rem(c, 2)
@@ -340,9 +342,8 @@
 
         queries_ready(c)
         stage_halo(c)
-        compute(c, edge_views, inner_views)
+        compute(c, edge_views, inner_views, lambda: finish(c - 1))
         send_out(ROWS, c)
-        finish(c - 1)
 
     finish(chunks - 1)
 
@@ -362,9 +363,7 @@
 def deliver(*refs):
     count = len(refs) // 2
     copies = [
-        pltpu.make_async_copy(refs[i].at[v], refs[count + i].at[v], refs[-1].at[i, v])
-        for i in range(count)
-        for v in range(refs[0].shape[0])
+        pltpu.make_async_copy(refs[i], refs[count + i], refs[-1].at[i]) for i in range(count)
     ]
     for copy in copies:
         copy.start()
@@ -415,7 +414,7 @@
             out_shape=(shape,) * 4,
             in_specs=[pl.BlockSpec(memory_space=pltpu.VMEM)] * 4,
             out_specs=[pl.BlockSpec(memory_space=pl.ANY)] * 4,
-            scratch_shapes=[dma((4, views))],
+            scratch_shapes=[dma((4,))],
             compiler_params=pltpu.CompilerParams(vmem_limit_bytes=48 * 1024 * 1024),
         )(*results)
 

time: 34.9 us -> 35.3 us (1.011)
  Pallas kernels: 34.1 us -> 34.5 us
    pallas_call x1, Pallas kernels: 32.9 us -> 33.4 us  [local(): pl.pallas_call(functools.partial(kernel, groups, parts), out_shape=(vmem(...]
where the time goes in v8:
time: 35.3 us; the launch traced here: 35.1 us
  Pallas kernels  34.5 us (98%)
  between operations  0.64 us (2%)
    pallas_call x1, Pallas kernels, local(): pl.pallas_call(functools.partial(kernel, groups, parts), out_shape=(vmem(...  33.4 us
    pallas_call x1, Pallas kernels, local(): pl.pallas_call(deliver, out_shape=(shape,) * 4, in_specs=[pl.BlockSpec(me...  1.11 us

profile of v8, /device:TPU:0, one launch (start us, length us, event | category | flops | bytes accessed | tf_op | source)
XLA Modules:
  0.0 35.1 jit_solution(2126447608546033967)
XLA Ops:
  0.6 33.4 %shard_map.75 = (bf16[3,49,1024]{2,1,0:T(8,128)(2,1)S(1)}, bf16[3,49,1024]{2,1,0:T(8,128)(2,1)S(1)}, bf16[3,49,1024]{2,1,0:T(8,128)(2,1)S(1)}, bf16[3,49,1024]{2,1,0:T(8,128)(2,1)S(1)}) custom-call(bf16[3,49,1024]{2,1,0:T(8,128)(2,1)} %q_ref.1, bf16[3,49,1024]{2,1,0:T(8,128)(2,1)} %k_ref.1, bf16[3,49,1024]{2,1,0:T(8,128)(2,1)} %v_ref.1, ...), custom_call_target="tpu_custom_call" | custom-call | flops 531062784 | bytes 2408448 | tf_op jit(solution)/shard_map/pallas_call | solution.py:393
  34.0 1.1 %shard_map.76 = (bf16[3,49,1024]{2,1,0:T(8,128)(2,1)}, bf16[3,49,1024]{2,1,0:T(8,128)(2,1)}, bf16[3,49,1024]{2,1,0:T(8,128)(2,1)}, bf16[3,49,1024]{2,1,0:T(8,128)(2,1)}) custom-call(bf16[3,49,1024]{2,1,0:T(8,128)(2,1)S(1)} %get-tuple-element.8.refs_0_, bf16[3,49,1024]{2,1,0:T(8,128)(2,1)S(1)} %get-tuple-element.9.refs_1_, ...), custom_call_target="tpu_custom_call" | custom-call | tf_op jit(solution)/shard_map/pallas_call | solution.py:412

commit v9 on v8

--- a/solution.py
+++ b/solution.py
@@ -134,15 +134,10 @@
         if kind == PAIRS:
             pl.semaphore_wait(barrier, parts + 1)
         send_in(kind, 0)
-    if chunks > 1:
-        send_in(PAIRS, 1)
 
     @pl.loop(1, chunks)
     def _(c):
-        @pl.when(c + 1 < chunks)
-        def _():
-            send_in(PAIRS, c + 1)
-
+        send_in(PAIRS, c)
         send_in(ROWS, c)
 
     for a in range(4):
@@ -322,6 +317,13 @@
                 send_out(PAIRS, c)
 
     tails[...] = jnp.zeros_like(tails)
+    def advance(c):
+        @pl.when(c + 1 < chunks)
+        def _():
+            relay(c + 1)
+
+        finish(c - 1)
+
     relay(0)
     clear(0)
     queries_ready(0)
@@ -336,13 +338,9 @@
     def _(c):
         clear(c)
 
-        @pl.when(c + 1 < chunks)
-        def _():
-            relay(c + 1)
-
         queries_ready(c)
         stage_halo(c)
-        compute(c, edge_views, inner_views, lambda: finish(c - 1))
+        compute(c, edge_views, inner_views, lambda: advance(c))
         send_out(ROWS, c)
 
     finish(chunks - 1)

time: 35.3 us -> 40.6 us (1.15)
  Pallas kernels: 34.5 us -> 39.8 us
    pallas_call x1, Pallas kernels: 33.4 us -> 38.7 us  [local(): pl.pallas_call(functools.partial(kernel, groups, parts), out_shape=(vmem(...]
where the time goes in v9:
time: 40.6 us; the launch traced here: 40.5 us
  Pallas kernels  39.8 us (98%)
  between operations  0.64 us (2%)
    pallas_call x1, Pallas kernels, local(): pl.pallas_call(functools.partial(kernel, groups, parts), out_shape=(vmem(...  38.7 us
    pallas_call x1, Pallas kernels, local(): pl.pallas_call(deliver, out_shape=(shape,) * 4, in_specs=[pl.BlockSpec(me...  1.11 us

profile of v9, /device:TPU:0, one launch (start us, length us, event | category | flops | bytes accessed | tf_op | source)
XLA Modules:
  0.0 40.5 jit_solution(17837060203296342536)
XLA Ops:
  0.6 38.7 %shard_map.75 = (bf16[3,49,1024]{2,1,0:T(8,128)(2,1)S(1)}, bf16[3,49,1024]{2,1,0:T(8,128)(2,1)S(1)}, bf16[3,49,1024]{2,1,0:T(8,128)(2,1)S(1)}, bf16[3,49,1024]{2,1,0:T(8,128)(2,1)S(1)}) custom-call(bf16[3,49,1024]{2,1,0:T(8,128)(2,1)} %q_ref.1, bf16[3,49,1024]{2,1,0:T(8,128)(2,1)} %k_ref.1, bf16[3,49,1024]{2,1,0:T(8,128)(2,1)} %v_ref.1, ...), custom_call_target="tpu_custom_call" | custom-call | flops 531062784 | bytes 2408448 | tf_op jit(solution)/shard_map/pallas_call | solution.py:391
  39.4 1.1 %shard_map.76 = (bf16[3,49,1024]{2,1,0:T(8,128)(2,1)}, bf16[3,49,1024]{2,1,0:T(8,128)(2,1)}, bf16[3,49,1024]{2,1,0:T(8,128)(2,1)}, bf16[3,49,1024]{2,1,0:T(8,128)(2,1)}) custom-call(bf16[3,49,1024]{2,1,0:T(8,128)(2,1)S(1)} %get-tuple-element.8.refs_0_, bf16[3,49,1024]{2,1,0:T(8,128)(2,1)S(1)} %get-tuple-element.9.refs_1_, ...), custom_call_target="tpu_custom_call" | custom-call | tf_op jit(solution)/shard_map/pallas_call | solution.py:410
